TPU v7x, 32 devices: a whole 2x2x4 slice. The times are simulated.
32 devices in a mesh: lat: 8 (over z, x), lev: 4 (over y, core).
Axes of the slice: x: 2, y: 2, z: 4, core: 2. Of those that a mesh axis runs over, the one named last changes fastest.
Arguments:
- spectral: bfloat16 [1280, 1280, 64], P('lat', 'lev'), may hold values from -0.0048828125 to 0.0048828125
- legendre: bfloat16 [1280, 1280, 32], P('lat', 'lev'), may hold values from -6 to 6
- weights: float32 [16], P('lat'), may hold values from 4 to 40
- points: int32 [8], P('lat'), may hold values from 20 to 5136, as said below
- assignment: int32 [1280], replicated, may hold values from 0 to 1279, each once
Outputs:
- tendency: bfloat16 [1280, 1280, 64], P('lat', 'lev')
- grid_values: bfloat16 [16, 8, 4, 5376], P('lat', 'lev')
Inputs may be any that keep to these rules, and one draw needn't show every extreme that they name: `assignment`: each of the 1280 wavenumbers appears once; slot k lies with lat index k // 160. `points`: each value is 20 + 4 i for a row index i from 0 to 1279; some pair has 20 points and some pair 4 * 1280 + 16.
All inputs are finite; a program needn't handle non-finite values.
Results may differ from a plain program's by a relative error of at most 0.03.
Values may be sent and summed in bfloat16 or wider, within the bound.
A program may use at most 64 MiB of HBM per device.

v0:
```python
import math

import jax
import jax.numpy as jnp
from jax import lax
from jax.sharding import PartitionSpec as P

XBLOCK = 256
NPAD = 5376


def angle_parts(wavenums, row_points, columns):
    residue = wavenums[:, None] * columns[None, :] % row_points
    angles = residue.astype(jnp.float32) * (2.0 * math.pi / row_points.astype(jnp.float32))
    return (jnp.cos(angles), jnp.sin(angles))


def block_table(wavenums, row_points, first_column, base_cos, base_sin):
    width = base_cos.shape[1]
    columns = first_column + jnp.arange(width, dtype=jnp.int32)
    start_cos, start_sin = angle_parts(wavenums, row_points, jnp.reshape(first_column, (1,)))
    cosine_vals = start_cos * base_cos - start_sin * base_sin
    sine_vals = start_sin * base_cos + start_cos * base_sin
    active = (2 * wavenums[:, None] < row_points) & (columns[None, :] < row_points)
    cosine_rows = jnp.where(active, cosine_vals, 0.0).astype(jnp.bfloat16)
    sine_rows = jnp.where(active, sine_vals, 0.0).astype(jnp.bfloat16)
    return jnp.concatenate([cosine_rows, sine_rows], axis=0)


def inverse_coefs(real_value, imag_value, real_slope, imag_slope, wavenums):
    truncation = wavenums.shape[0]
    factor = jnp.where(wavenums == 0, 1.0, 2.0).astype(jnp.float32)
    scaled_m = wavenums.astype(jnp.float32) / truncation
    cosine_part = jnp.stack(
        [factor * real_value, -factor * scaled_m * imag_value, factor * real_slope], axis=1
    )
    sine_part = jnp.stack(
        [-factor * imag_value, -factor * scaled_m * real_value, -factor * imag_slope], axis=1
    )
    return jnp.concatenate([cosine_part, sine_part], axis=-1).astype(jnp.bfloat16)


def grid_products(grid_field, scales):
    value_field = grid_field[:, 0]
    zonal_slope = grid_field[:, 1]
    merid_slope = grid_field[:, 2]
    advect = (
        jnp.roll(value_field, -1, axis=2) * zonal_slope
        + jnp.roll(value_field, -2, axis=2) * merid_slope
    )
    product = value_field * jnp.roll(value_field, -3, axis=2)
    terms = jnp.stack([advect, product], axis=1) * scales[:, None, None, None, None]
    return (value_field.astype(jnp.bfloat16), terms.astype(jnp.bfloat16))


def direct_parts(spectra, wave_count):
    real_part = spectra[:, :wave_count]
    imag_part = -spectra[:, wave_count:]
    shape_out = (2, 2, -1, 4, wave_count)
    return jnp.stack([real_part.reshape(shape_out), imag_part.reshape(shape_out)], axis=3).astype(
        jnp.bfloat16
    )


def make_term(source, legendre):
    return jnp.einsum("knc,knt->ckt", source, legendre, preferred_element_type=jnp.float32)


def body(spectral, legendre, weights, points, assignment):
    own_slots, own_totals, column_count = spectral.shape
    wave_count = assignment.shape[0]
    levels = column_count // 8
    local_levels = levels // lax.axis_size("lev")
    pair_count = points.shape[0]
    own_waves = lax.dynamic_slice_in_dim(assignment, lax.axis_index("lat") * own_slots, own_slots)
    totals = lax.axis_index("lev") * own_totals + jnp.arange(own_totals, dtype=jnp.int32)
    triangle = totals[None, :] >= own_waves[:, None]
    masked = jnp.where(triangle[:, :, None], spectral, jnp.zeros((), spectral.dtype))
    summed = lax.psum_scatter(
        make_term(masked, legendre).astype(jnp.bfloat16), "lev", scatter_dimension=0, tiled=True
    ).astype(jnp.float32)
    fourier = lax.all_to_all(
        summed.astype(jnp.bfloat16), "lat", split_axis=2, concat_axis=1, tiled=True
    ).astype(summed.dtype)
    grouped = fourier.reshape(local_levels, 2, 4, wave_count, pair_count, 2, 2)
    block_count = NPAD // XBLOCK
    row_points = points[0]
    components = grouped[:, :, :, :, 0]

    def select(deriv, half):
        return jnp.moveaxis(components[:, half, :, :, :, deriv], -1, 0)

    coefs = inverse_coefs(select(0, 0), select(0, 1), select(1, 0), select(1, 1), assignment)
    coefs = coefs.reshape(-1, 2 * wave_count)
    scales = weights / row_points.astype(jnp.float32)
    base_cos, base_sin = angle_parts(assignment, row_points, jnp.arange(XBLOCK, dtype=jnp.int32))

    def block_step(running, block_index):
        basis = block_table(assignment, row_points, block_index * XBLOCK, base_cos, base_sin)
        grid_field = jnp.dot(coefs, basis, preferred_element_type=jnp.float32)
        grid_field = grid_field.reshape(2, 3, local_levels, 4, XBLOCK)
        values, terms = grid_products(grid_field, scales)
        running = running + lax.dot_general(
            terms.reshape(-1, XBLOCK),
            basis,
            (((1,), (1,)), ((), ())),
            preferred_element_type=jnp.float32,
        )
        return (running, values)

    start_sums = jnp.zeros((16 * local_levels, 2 * wave_count), jnp.float32)
    spectra, values = lax.scan(block_step, start_sums, jnp.arange(block_count, dtype=jnp.int32))
    values = jnp.moveaxis(values, 0, 3).reshape(2, local_levels, 4, NPAD)
    wave_data = direct_parts(spectra, wave_count)
    waves_all = [jnp.transpose(wave_data, (2, 3, 4, 5, 0, 1))]
    local_waves = jnp.stack(waves_all, axis=4).reshape(local_levels, 2, 4, wave_count, -1)
    spread = lax.all_to_all(
        local_waves.reshape(8 * local_levels, wave_count, -1),
        "lat",
        split_axis=1,
        concat_axis=2,
        tiled=True,
    )
    result = jnp.einsum(
        "knt,ckt->knc",
        legendre,
        lax.all_gather(spread, "lev", axis=0, tiled=True),
        preferred_element_type=jnp.float32,
    )
    tendency = jnp.where(triangle[:, :, None], result, 0.0).astype(jnp.bfloat16)
    return (tendency, values)


def solution(mesh):
    in_specs = (P("lat", "lev", None), P("lat", "lev", None), P("lat"), P("lat"), P())
    out_specs = (P("lat", "lev", None), P("lat", "lev", None, None))
    return jax.shard_map(body, mesh=mesh, in_specs=in_specs, out_specs=out_specs, check_vma=False)
```

profile of v0, /device:TPU:0, one launch (start us, length us, event | category | flops | bytes accessed | tf_op | source)
XLA Modules:
  0.0 593.4 jit_solution(15113674196936624574)
XLA Ops:
  7.2 0.8 dynamic_slice.9
  8.1 7.2 %fusion.40 = bf16[64,160,32]{0,2,1:T(8,128)(2,1)S(1)} fusion(bf16[160,320,32]{1,2,0:T(8,128)(2,1)} %param.8, bf16[160,320,64]{1,2,0:T(8,128)(2,1)} %param.7, pred[160,320]{1,0:T(8,128)(4,1)S(1)} %broadcast_compare_fusion), kind=kOutput, calls=%fused_computation.61 | convolution fusion | flops 213319680 | bytes 10536960 | tf_op jit(solution)/shard_map/knc,knt->ckt/dot_general | solution.py:66
  15.3 3.0 copy.50
  19.0 27.1 %reduce-scatter.2.cloned.1.call-done = bf16[16,160,32]{1,2,0:T(8,128)(2,1)} async-done(((bf16[64,160,32]{1,2,0:T(8,128)(2,1)}), bf16[16,160,32]{1,2,0:T(8,128)(2,1)}) %reduce-scatter.2.cloned.1.call-update) | async-done | bytes 163856 | tf_op jit(solution)/shard_map/reduce_scatter | solution.py:79
  46.0 1.8 copy.51
  47.8 5.5 all-to-all-start
  53.5 8.8 %all-to-all-done = bf16[16,160,32]{1,0,2:T(8,128)(2,1)S(1)} async-done(((bf16[16,160,32]{1,0,2:T(8,128)(2,1)}), bf16[16,160,32]{1,0,2:T(8,128)(2,1)S(1)}, u32[]{:S(2)}, u32[]{:S(2)}) %all-to-all-start) | async-done | bytes 163872 | tf_op jit(solution)/shard_map/all_to_all | solution.py:82
  64.0 481.7 %while.17 = (s32[]{:T(128)}, f32[32,2560]{1,0:T(8,128)S(1)}, bf16[21,2,2,4,256]{4,3,2,1,0:T(4,128)(2,1)S(1)}, s32[1280]{0:T(1024)S(1)}, s32[]{:T(128)}, /*index=...) while((s32[]{:T(128)}, f32[32,2560]{1,0:T(8,128)S(1)}, ...), condition=%wide.region_2.3_spmd.clone.clone.clone, body=%wide.region_1.2_spmd.clone.clone.clone.sunk | while | flops 117214720 | bytes 5528285 | solution.py:112
  65.3 0.7 add_compare_fusion.2
  67.0 19.0 %fusion.66 = (bf16[1280,256]{1,0:T(8,128)(2,1)S(1)}, bf16[1280,256]{1,0:T(8,128)(2,1)S(1)}) fusion(f32[]{:T(128)} %get-tuple-element.448, s32[]{:T(128)} %get-tuple-element.446, s32[1280]{0:T(1024)S(1)} %get-tuple-element.443, f32[1280]{0:T(1024)S(1)} %get-tuple-element.400, f32[1280]{0:T(1024)S(1)} %get-tuple-element.401, pred[]{:T(512)} %get-tuple-element.447, ...), kind=kLoop, calls=%fused_computation.6.clone.1 | loop fusion | flops 6881280 | bytes 1327625 | tf_op jit(solution)/shard_map/while/body/eval_jaxpr/convert_element_type | solution.py:25
  88.2 0.7 add_compare_fusion.2
  88.9 0.7 multiply_compare_fusion.2
  89.9 19.0 %fusion.66 = (bf16[1280,256]{1,0:T(8,128)(2,1)S(1)}, bf16[1280,256]{1,0:T(8,128)(2,1)S(1)}) fusion(f32[]{:T(128)} %get-tuple-element.448, s32[]{:T(128)} %get-tuple-element.446, s32[1280]{0:T(1024)S(1)} %get-tuple-element.443, f32[1280]{0:T(1024)S(1)} %get-tuple-element.400, f32[1280]{0:T(1024)S(1)} %get-tuple-element.401, pred[]{:T(512)} %get-tuple-element.447, ...), kind=kLoop, calls=%fused_computation.6.clone.1 | loop fusion | flops 6881280 | bytes 1327625 | tf_op jit(solution)/shard_map/while/body/eval_jaxpr/convert_element_type | solution.py:25
  111.2 0.7 add_compare_fusion.2
  111.8 0.7 multiply_compare_fusion.2
  112.8 19.0 %fusion.66 = (bf16[1280,256]{1,0:T(8,128)(2,1)S(1)}, bf16[1280,256]{1,0:T(8,128)(2,1)S(1)}) fusion(f32[]{:T(128)} %get-tuple-element.448, s32[]{:T(128)} %get-tuple-element.446, s32[1280]{0:T(1024)S(1)} %get-tuple-element.443, f32[1280]{0:T(1024)S(1)} %get-tuple-element.400, f32[1280]{0:T(1024)S(1)} %get-tuple-element.401, pred[]{:T(512)} %get-tuple-element.447, ...), kind=kLoop, calls=%fused_computation.6.clone.1 | loop fusion | flops 6881280 | bytes 1327625 | tf_op jit(solution)/shard_map/while/body/eval_jaxpr/convert_element_type | solution.py:25
  134.1 0.7 add_compare_fusion.2
  134.8 0.7 multiply_compare_fusion.2
  135.8 19.0 %fusion.66 = (bf16[1280,256]{1,0:T(8,128)(2,1)S(1)}, bf16[1280,256]{1,0:T(8,128)(2,1)S(1)}) fusion(f32[]{:T(128)} %get-tuple-element.448, s32[]{:T(128)} %get-tuple-element.446, s32[1280]{0:T(1024)S(1)} %get-tuple-element.443, f32[1280]{0:T(1024)S(1)} %get-tuple-element.400, f32[1280]{0:T(1024)S(1)} %get-tuple-element.401, pred[]{:T(512)} %get-tuple-element.447, ...), kind=kLoop, calls=%fused_computation.6.clone.1 | loop fusion | flops 6881280 | bytes 1327625 | tf_op jit(solution)/shard_map/while/body/eval_jaxpr/convert_element_type | solution.py:25
  157.0 0.7 add_compare_fusion.2
  157.7 0.7 multiply_compare_fusion.2
  158.7 19.0 %fusion.66 = (bf16[1280,256]{1,0:T(8,128)(2,1)S(1)}, bf16[1280,256]{1,0:T(8,128)(2,1)S(1)}) fusion(f32[]{:T(128)} %get-tuple-element.448, s32[]{:T(128)} %get-tuple-element.446, s32[1280]{0:T(1024)S(1)} %get-tuple-element.443, f32[1280]{0:T(1024)S(1)} %get-tuple-element.400, f32[1280]{0:T(1024)S(1)} %get-tuple-element.401, pred[]{:T(512)} %get-tuple-element.447, ...), kind=kLoop, calls=%fused_computation.6.clone.1 | loop fusion | flops 6881280 | bytes 1327625 | tf_op jit(solution)/shard_map/while/body/eval_jaxpr/convert_element_type | solution.py:25
  180.0 0.7 add_compare_fusion.2
  180.6 0.7 multiply_compare_fusion.2
  181.6 19.0 %fusion.66 = (bf16[1280,256]{1,0:T(8,128)(2,1)S(1)}, bf16[1280,256]{1,0:T(8,128)(2,1)S(1)}) fusion(f32[]{:T(128)} %get-tuple-element.448, s32[]{:T(128)} %get-tuple-element.446, s32[1280]{0:T(1024)S(1)} %get-tuple-element.443, f32[1280]{0:T(1024)S(1)} %get-tuple-element.400, f32[1280]{0:T(1024)S(1)} %get-tuple-element.401, pred[]{:T(512)} %get-tuple-element.447, ...), kind=kLoop, calls=%fused_computation.6.clone.1 | loop fusion | flops 6881280 | bytes 1327625 | tf_op jit(solution)/shard_map/while/body/eval_jaxpr/convert_element_type | solution.py:25
  203.6 0.7 multiply_compare_fusion.2
  204.6 19.0 %fusion.66 = (bf16[1280,256]{1,0:T(8,128)(2,1)S(1)}, bf16[1280,256]{1,0:T(8,128)(2,1)S(1)}) fusion(f32[]{:T(128)} %get-tuple-element.448, s32[]{:T(128)} %get-tuple-element.446, s32[1280]{0:T(1024)S(1)} %get-tuple-element.443, f32[1280]{0:T(1024)S(1)} %get-tuple-element.400, f32[1280]{0:T(1024)S(1)} %get-tuple-element.401, pred[]{:T(512)} %get-tuple-element.447, ...), kind=kLoop, calls=%fused_computation.6.clone.1 | loop fusion | flops 6881280 | bytes 1327625 | tf_op jit(solution)/shard_map/while/body/eval_jaxpr/convert_element_type | solution.py:25
  225.9 0.7 add_compare_fusion.2
  227.5 19.0 %fusion.66 = (bf16[1280,256]{1,0:T(8,128)(2,1)S(1)}, bf16[1280,256]{1,0:T(8,128)(2,1)S(1)}) fusion(f32[]{:T(128)} %get-tuple-element.448, s32[]{:T(128)} %get-tuple-element.446, s32[1280]{0:T(1024)S(1)} %get-tuple-element.443, f32[1280]{0:T(1024)S(1)} %get-tuple-element.400, f32[1280]{0:T(1024)S(1)} %get-tuple-element.401, pred[]{:T(512)} %get-tuple-element.447, ...), kind=kLoop, calls=%fused_computation.6.clone.1 | loop fusion | flops 6881280 | bytes 1327625 | tf_op jit(solution)/shard_map/while/body/eval_jaxpr/convert_element_type | solution.py:25
  248.8 0.7 add_compare_fusion.2
  249.5 0.7 multiply_compare_fusion.2
  250.5 19.0 %fusion.66 = (bf16[1280,256]{1,0:T(8,128)(2,1)S(1)}, bf16[1280,256]{1,0:T(8,128)(2,1)S(1)}) fusion(f32[]{:T(128)} %get-tuple-element.448, s32[]{:T(128)} %get-tuple-element.446, s32[1280]{0:T(1024)S(1)} %get-tuple-element.443, f32[1280]{0:T(1024)S(1)} %get-tuple-element.400, f32[1280]{0:T(1024)S(1)} %get-tuple-element.401, pred[]{:T(512)} %get-tuple-element.447, ...), kind=kLoop, calls=%fused_computation.6.clone.1 | loop fusion | flops 6881280 | bytes 1327625 | tf_op jit(solution)/shard_map/while/body/eval_jaxpr/convert_element_type | solution.py:25
  271.7 0.7 add_compare_fusion.2
  272.4 0.7 multiply_compare_fusion.2
  273.4 19.0 %fusion.66 = (bf16[1280,256]{1,0:T(8,128)(2,1)S(1)}, bf16[1280,256]{1,0:T(8,128)(2,1)S(1)}) fusion(f32[]{:T(128)} %get-tuple-element.448, s32[]{:T(128)} %get-tuple-element.446, s32[1280]{0:T(1024)S(1)} %get-tuple-element.443, f32[1280]{0:T(1024)S(1)} %get-tuple-element.400, f32[1280]{0:T(1024)S(1)} %get-tuple-element.401, pred[]{:T(512)} %get-tuple-element.447, ...), kind=kLoop, calls=%fused_computation.6.clone.1 | loop fusion | flops 6881280 | bytes 1327625 | tf_op jit(solution)/shard_map/while/body/eval_jaxpr/convert_element_type | solution.py:25
  294.7 0.7 add_compare_fusion.2
  295.3 0.7 multiply_compare_fusion.2
  296.3 19.0 %fusion.66 = (bf16[1280,256]{1,0:T(8,128)(2,1)S(1)}, bf16[1280,256]{1,0:T(8,128)(2,1)S(1)}) fusion(f32[]{:T(128)} %get-tuple-element.448, s32[]{:T(128)} %get-tuple-element.446, s32[1280]{0:T(1024)S(1)} %get-tuple-element.443, f32[1280]{0:T(1024)S(1)} %get-tuple-element.400, f32[1280]{0:T(1024)S(1)} %get-tuple-element.401, pred[]{:T(512)} %get-tuple-element.447, ...), kind=kLoop, calls=%fused_computation.6.clone.1 | loop fusion | flops 6881280 | bytes 1327625 | tf_op jit(solution)/shard_map/while/body/eval_jaxpr/convert_element_type | solution.py:25
  317.6 0.7 add_compare_fusion.2
  318.3 0.7 multiply_compare_fusion.2
  319.3 19.0 %fusion.66 = (bf16[1280,256]{1,0:T(8,128)(2,1)S(1)}, bf16[1280,256]{1,0:T(8,128)(2,1)S(1)}) fusion(f32[]{:T(128)} %get-tuple-element.448, s32[]{:T(128)} %get-tuple-element.446, s32[1280]{0:T(1024)S(1)} %get-tuple-element.443, f32[1280]{0:T(1024)S(1)} %get-tuple-element.400, f32[1280]{0:T(1024)S(1)} %get-tuple-element.401, pred[]{:T(512)} %get-tuple-element.447, ...), kind=kLoop, calls=%fused_computation.6.clone.1 | loop fusion | flops 6881280 | bytes 1327625 | tf_op jit(solution)/shard_map/while/body/eval_jaxpr/convert_element_type | solution.py:25
  340.6 0.7 add_compare_fusion.2
  341.2 0.7 multiply_compare_fusion.2
  342.2 19.0 %fusion.66 = (bf16[1280,256]{1,0:T(8,128)(2,1)S(1)}, bf16[1280,256]{1,0:T(8,128)(2,1)S(1)}) fusion(f32[]{:T(128)} %get-tuple-element.448, s32[]{:T(128)} %get-tuple-element.446, s32[1280]{0:T(1024)S(1)} %get-tuple-element.443, f32[1280]{0:T(1024)S(1)} %get-tuple-element.400, f32[1280]{0:T(1024)S(1)} %get-tuple-element.401, pred[]{:T(512)} %get-tuple-element.447, ...), kind=kLoop, calls=%fused_computation.6.clone.1 | loop fusion | flops 6881280 | bytes 1327625 | tf_op jit(solution)/shard_map/while/body/eval_jaxpr/convert_element_type | solution.py:25
  363.5 0.7 add_compare_fusion.2
  364.2 0.7 multiply_compare_fusion.2
  365.2 19.0 %fusion.66 = (bf16[1280,256]{1,0:T(8,128)(2,1)S(1)}, bf16[1280,256]{1,0:T(8,128)(2,1)S(1)}) fusion(f32[]{:T(128)} %get-tuple-element.448, s32[]{:T(128)} %get-tuple-element.446, s32[1280]{0:T(1024)S(1)} %get-tuple-element.443, f32[1280]{0:T(1024)S(1)} %get-tuple-element.400, f32[1280]{0:T(1024)S(1)} %get-tuple-element.401, pred[]{:T(512)} %get-tuple-element.447, ...), kind=kLoop, calls=%fused_computation.6.clone.1 | loop fusion | flops 6881280 | bytes 1327625 | tf_op jit(solution)/shard_map/while/body/eval_jaxpr/convert_element_type | solution.py:25
  388.1 19.0 %fusion.66 = (bf16[1280,256]{1,0:T(8,128)(2,1)S(1)}, bf16[1280,256]{1,0:T(8,128)(2,1)S(1)}) fusion(f32[]{:T(128)} %get-tuple-element.448, s32[]{:T(128)} %get-tuple-element.446, s32[1280]{0:T(1024)S(1)} %get-tuple-element.443, f32[1280]{0:T(1024)S(1)} %get-tuple-element.400, f32[1280]{0:T(1024)S(1)} %get-tuple-element.401, pred[]{:T(512)} %get-tuple-element.447, ...), kind=kLoop, calls=%fused_computation.6.clone.1 | loop fusion | flops 6881280 | bytes 1327625 | tf_op jit(solution)/shard_map/while/body/eval_jaxpr/convert_element_type | solution.py:25
  411.0 19.0 %fusion.66 = (bf16[1280,256]{1,0:T(8,128)(2,1)S(1)}, bf16[1280,256]{1,0:T(8,128)(2,1)S(1)}) fusion(f32[]{:T(128)} %get-tuple-element.448, s32[]{:T(128)} %get-tuple-element.446, s32[1280]{0:T(1024)S(1)} %get-tuple-element.443, f32[1280]{0:T(1024)S(1)} %get-tuple-element.400, f32[1280]{0:T(1024)S(1)} %get-tuple-element.401, pred[]{:T(512)} %get-tuple-element.447, ...), kind=kLoop, calls=%fused_computation.6.clone.1 | loop fusion | flops 6881280 | bytes 1327625 | tf_op jit(solution)/shard_map/while/body/eval_jaxpr/convert_element_type | solution.py:25
  434.0 19.0 %fusion.66 = (bf16[1280,256]{1,0:T(8,128)(2,1)S(1)}, bf16[1280,256]{1,0:T(8,128)(2,1)S(1)}) fusion(f32[]{:T(128)} %get-tuple-element.448, s32[]{:T(128)} %get-tuple-element.446, s32[1280]{0:T(1024)S(1)} %get-tuple-element.443, f32[1280]{0:T(1024)S(1)} %get-tuple-element.400, f32[1280]{0:T(1024)S(1)} %get-tuple-element.401, pred[]{:T(512)} %get-tuple-element.447, ...), kind=kLoop, calls=%fused_computation.6.clone.1 | loop fusion | flops 6881280 | bytes 1327625 | tf_op jit(solution)/shard_map/while/body/eval_jaxpr/convert_element_type | solution.py:25
  456.9 19.0 %fusion.66 = (bf16[1280,256]{1,0:T(8,128)(2,1)S(1)}, bf16[1280,256]{1,0:T(8,128)(2,1)S(1)}) fusion(f32[]{:T(128)} %get-tuple-element.448, s32[]{:T(128)} %get-tuple-element.446, s32[1280]{0:T(1024)S(1)} %get-tuple-element.443, f32[1280]{0:T(1024)S(1)} %get-tuple-element.400, f32[1280]{0:T(1024)S(1)} %get-tuple-element.401, pred[]{:T(512)} %get-tuple-element.447, ...), kind=kLoop, calls=%fused_computation.6.clone.1 | loop fusion | flops 6881280 | bytes 1327625 | tf_op jit(solution)/shard_map/while/body/eval_jaxpr/convert_element_type | solution.py:25
  479.8 19.0 %fusion.66 = (bf16[1280,256]{1,0:T(8,128)(2,1)S(1)}, bf16[1280,256]{1,0:T(8,128)(2,1)S(1)}) fusion(f32[]{:T(128)} %get-tuple-element.448, s32[]{:T(128)} %get-tuple-element.446, s32[1280]{0:T(1024)S(1)} %get-tuple-element.443, f32[1280]{0:T(1024)S(1)} %get-tuple-element.400, f32[1280]{0:T(1024)S(1)} %get-tuple-element.401, pred[]{:T(512)} %get-tuple-element.447, ...), kind=kLoop, calls=%fused_computation.6.clone.1 | loop fusion | flops 6881280 | bytes 1327625 | tf_op jit(solution)/shard_map/while/body/eval_jaxpr/convert_element_type | solution.py:25
  502.8 19.0 %fusion.66 = (bf16[1280,256]{1,0:T(8,128)(2,1)S(1)}, bf16[1280,256]{1,0:T(8,128)(2,1)S(1)}) fusion(f32[]{:T(128)} %get-tuple-element.448, s32[]{:T(128)} %get-tuple-element.446, s32[1280]{0:T(1024)S(1)} %get-tuple-element.443, f32[1280]{0:T(1024)S(1)} %get-tuple-element.400, f32[1280]{0:T(1024)S(1)} %get-tuple-element.401, pred[]{:T(512)} %get-tuple-element.447, ...), kind=kLoop, calls=%fused_computation.6.clone.1 | loop fusion | flops 6881280 | bytes 1327625 | tf_op jit(solution)/shard_map/while/body/eval_jaxpr/convert_element_type | solution.py:25
  525.7 19.0 %fusion.66 = (bf16[1280,256]{1,0:T(8,128)(2,1)S(1)}, bf16[1280,256]{1,0:T(8,128)(2,1)S(1)}) fusion(f32[]{:T(128)} %get-tuple-element.448, s32[]{:T(128)} %get-tuple-element.446, s32[1280]{0:T(1024)S(1)} %get-tuple-element.443, f32[1280]{0:T(1024)S(1)} %get-tuple-element.400, f32[1280]{0:T(1024)S(1)} %get-tuple-element.401, pred[]{:T(512)} %get-tuple-element.447, ...), kind=kLoop, calls=%fused_computation.6.clone.1 | loop fusion | flops 6881280 | bytes 1327625 | tf_op jit(solution)/shard_map/while/body/eval_jaxpr/convert_element_type | solution.py:25
  546.0 0.8 copy.60
  546.8 2.0 reshape.152
  548.9 3.6 all-to-all-start.1
  552.4 0.7 copy.74
  553.2 6.8 %all-to-all-done.1 = bf16[8,2,5120]{2,1,0:T(2,128)(2,1)S(1)} async-done(((bf16[8,2,5120]{2,1,0:T(2,128)(2,1)}), bf16[8,2,5120]{2,1,0:T(2,128)(2,1)S(1)}, u32[]{:S(2)}, u32[]{:S(2)}) %all-to-all-start.1) | async-done | bytes 163872 | tf_op jit(solution)/shard_map/all_to_all | solution.py:117
  560.0 0.9 reshape.153
  560.9 0.7 copy.66
  561.7 0.7 copy.63
  562.4 17.7 %all_gather.3 = bf16[64,160,32]{2,0,1:T(8,128)(2,1)S(1)} all-gather(bf16[16,160,32]{2,0,1:T(8,128)(2,1)S(1)} %copy.63), channel_id=1, replica_groups=mesh['lat'=8,'lev'=4] {'lev'}, dimensions={0}, use_global_device_ids=true | all-gather | bytes 819200 | tf_op jit(solution)/shard_map/all_gather | solution.py:127
  580.1 6.5 %fusion.35 = bf16[160,320,64]{1,2,0:T(8,128)(2,1)} fusion(bf16[64,160,32]{2,0,1:T(8,128)(2,1)S(1)} %all_gather.3, bf16[160,320,32]{1,2,0:T(8,128)(2,1)} %param.8, pred[160,320]{1,0:T(8,128)(4,1)S(1)} %broadcast_compare_fusion), kind=kOutput, calls=%fused_computation.58 | convolution fusion | flops 216268800 | bytes 10536960 | tf_op jit(solution)/shard_map/knt,ckt->knc/dot_general | solution.py:124
  (382 shorter events, 52.7 us)
Async XLA Ops:
  7.2 38.9 %reduce-scatter.2.cloned.1.call-start = ((), (), s32[]{:S(2)}) async-start(), calls=%async_computation.3 | async-start | bytes 1310720 | tf_op jit(solution)/shard_map/reduce_scatter | solution.py:79
  18.3 35.1 %copy-start.1 = (f32[2]{0:T(128)S(1)}, f32[2]{0:T(128)}, u32[]{:S(2)}) copy-start(f32[2]{0:T(128)} %param.9) | copy-start | bytes 28
  18.3 35.2 %copy-start = (s32[1280]{0:T(1024)S(1)}, s32[1280]{0:T(1024)}, u32[]{:S(2)}) copy-start(s32[1280]{0:T(1024)} %param.11) | copy-start | bytes 15364
  47.8 14.4 %all-to-all-start = ((bf16[16,160,32]{1,0,2:T(8,128)(2,1)}), bf16[16,160,32]{1,0,2:T(8,128)(2,1)S(1)}, u32[]{:S(2)}, u32[]{:S(2)}) async-start(bf16[16,160,32]{1,0,2:T(8,128)(2,1)} %copy.51), calls=%async_computation.1 | async-start | bytes 524288 | tf_op jit(solution)/shard_map/all_to_all | solution.py:82
  548.9 11.2 %all-to-all-start.1 = ((bf16[8,2,5120]{2,1,0:T(2,128)(2,1)}), bf16[8,2,5120]{2,1,0:T(2,128)(2,1)S(1)}, u32[]{:S(2)}, u32[]{:S(2)}) async-start(bf16[8,2,5120]{2,1,0:T(2,128)(2,1)} %reshape.152), calls=%async_computation.2 | async-start | bytes 327680 | tf_op jit(solution)/shard_map/all_to_all | solution.py:117
Sparse Core Ops, SparseCore 0:
  18.4 27.5 reduce-scatter.1
where the time goes:
time: 594 us; the launch traced here: 593 us
  other arithmetic  431 us (73%)
  waiting for transfers between devices  42.7 us (7%)
  matrix products  31.2 us (5%)
  local copies, waits for them, and re-layouts  30 us (5%)
  blocking collectives  17.7 us (3%)
  loops' own time  16.4 us (3%)
  between operations  14.9 us (3%)
  starting transfers between devices  9.14 us (2%)
    convert_element_type x21, other arithmetic, block_table(): cosine_rows = jnp.where(active, cosine_vals, 0.0).astype(jnp.bfloat16)  398 us
    reduce_scatter x1, waiting for transfers between devices, body(): lax.psum_scatter(make_term(masked, legendre).astype(jnp.bfloat16), 'lev',...  27.1 us
    all_gather x1, blocking collectives, body(): lax.all_gather(spread, 'lev', axis=0, tiled=True)  17.7 us
    another operation x1, loops' own time, body(): lax.scan(block_step, start_sums, jnp.arange(block_count, dtype=jnp.int32))  16.4 us
    lt x21, other arithmetic, block_table(): columns[None, :] < row_points  13.7 us
    lt x21, other arithmetic, block_table(): 2 * wavenums[:, None] < row_points  13.7 us
    dynamic_slice x21, local copies, waits for them, and re-layouts, body(): lax.scan(block_step, start_sums, jnp.arange(block_count, dtype=jnp.int32))  12.3 us
  transfers between devices with their start and end apart: 3, of which 3 were waited for; matrix products, arithmetic and copies ran while one was open for 0% of the time, Pallas kernels for 0%

commit v1 on v0

v1 whole, which is shorter than its diff:
```python
import math

import jax
import jax.numpy as jnp
from jax import lax
from jax.experimental import pallas as pl
from jax.experimental.pallas import tpu as pltpu
from jax.sharding import PartitionSpec as P

NPAD = 5376
LANE = 128


def sincos(product, quarter, step):
    turns = jnp.floor(product * (1.0 / quarter) + 0.5)
    theta = (product - turns * quarter) * step
    square = theta * theta
    sine = theta * (1.0 + square * (-1.0 / 6 + square * (1.0 / 120 - square * (1.0 / 5040))))
    cosine = 1.0 + square * (-0.5 + square * (1.0 / 24 + square * (-1.0 / 720 + square * (1.0 / 40320))))
    quadrant = turns.astype(jnp.int32) & 3
    odd = (quadrant & 1) == 1
    first = jnp.where(odd, sine, cosine)
    second = jnp.where(odd, cosine, sine)
    return (
        jnp.where((quadrant == 1) | (quadrant == 2), -first, first),
        jnp.where(quadrant >= 2, -second, second),
    )


def shift_field(rows, shift):
    count = rows.shape[0]
    field = lax.broadcasted_iota(jnp.int32, rows.shape, 0) % 4
    return jnp.where(
        field < 4 - shift,
        pltpu.roll(rows, count - shift, axis=0),
        pltpu.roll(rows, 4 - shift, axis=0),
    )


def grid_kernel(
    points_ref, scales_ref, waves_ref, four_ref, out_ref, values_ref,
    base_cos, base_sin, start_cos, start_sin, cos_tab, sin_tab, lhs_cos, lhs_sin, term_cos, term_sin, images,
):
    width = cos_tab.shape[0]
    wave_count = cos_tab.shape[1]
    rows = four_ref.shape[1]
    blocks = width // LANE
    row_points = points_ref[0]
    quarter_int = row_points // 4
    quarter = quarter_int.astype(jnp.float32)
    step = (0.5 * math.pi) / quarter
    m_int = waves_ref[...]
    m_float = m_int.astype(jnp.float32)

    def start_rows(count, scale):
        return (lax.broadcasted_iota(jnp.int32, (count, 1), 0) * scale).astype(jnp.float32)

    start_cos[...], start_sin[...] = sincos(start_rows(start_cos.shape[0], LANE) * m_float, quarter, step)

    @pl.loop(0, LANE // 8)
    def _(index):
        at = pl.multiple_of(index * 8, 8)
        offsets = (lax.broadcasted_iota(jnp.int32, (8, 1), 0) + at).astype(jnp.float32)
        base_cos[pl.ds(at, 8), :], base_sin[pl.ds(at, 8), :] = sincos(offsets * m_float, quarter, step)

    @pl.loop(0, width // 16)
    def _(index):
        at = pl.multiple_of(index * 16, 16)
        low = pl.multiple_of((index % (LANE // 16)) * 16, 16)
        start = index // (LANE // 16)
        for col in range(0, wave_count, 2 * LANE):
            cols = pl.ds(col, 2 * LANE)
            bc = base_cos[pl.ds(low, 16), cols]
            bs = base_sin[pl.ds(low, 16), cols]
            sc = start_cos[pl.ds(start, 1), cols]
            ss = start_sin[pl.ds(start, 1), cols]
            cos_tab[pl.ds(at, 16), cols] = (sc * bc - ss * bs).astype(jnp.bfloat16)
            sin_tab[pl.ds(at, 16), cols] = (ss * bc + sc * bs).astype(jnp.bfloat16)

    active = 2 * m_int < row_points
    parity = jnp.where((m_int & 1) == 0, 1.0, -1.0)
    factor = jnp.where(active, jnp.where(m_int == 0, 1.0, 2.0), 0.0)
    slope = factor * (m_float * (1.0 / wave_count))
    real_value, imag_value = four_ref[0].astype(jnp.float32), four_ref[1].astype(jnp.float32)
    real_slope, imag_slope = four_ref[2].astype(jnp.float32), four_ref[3].astype(jnp.float32)

    def fill(lhs, value, zonal, merid):
        parts = [value, shift_field(value, 1), shift_field(value, 2), shift_field(value, 3), zonal, merid]
        for index, part in enumerate(parts):
            lhs[pl.ds(index * rows, rows), :] = part.astype(jnp.bfloat16)
            lhs[pl.ds((6 + index) * rows, rows), :] = (part * parity).astype(jnp.bfloat16)

    fill(lhs_cos, factor * real_value, -slope * imag_value, factor * real_slope)
    fill(lhs_sin, -factor * imag_value, -slope * real_value, -factor * imag_slope)
    scale = scales_ref[...]

    @pl.loop(0, blocks)
    def _(index):
        at = pl.multiple_of(index * LANE, LANE)
        contract = (((1,), (1,)), ((), ()))
        even = lax.dot_general(lhs_cos[...], cos_tab[pl.ds(at, LANE), :], contract, preferred_element_type=jnp.float32)
        odd = lax.dot_general(lhs_sin[...], sin_tab[pl.ds(at, LANE), :], contract, preferred_element_type=jnp.float32)
        place = lax.broadcasted_iota(jnp.int32, (1, LANE), 1) + at
        closed = place <= quarter_int
        inner = (place >= 1) & (place < quarter_int)
        half = 6 * rows
        fields = (
            (even[:half] + odd[:half], closed),
            (even[half:] + odd[half:], closed),
            (even[half:] - odd[half:], inner),
            (even[:half] - odd[:half], inner),
        )
        terms = []
        for image, (field, keep) in enumerate(fields):
            q0, q1, q2, q3, zonal, merid = (field[part * rows:(part + 1) * rows] for part in range(6))
            images[image, :, pl.ds(at, LANE)] = jnp.where(keep, q0, 0.0)
            weight = jnp.where(keep, scale, 0.0)
            terms.append(jnp.concatenate([(q1 * zonal + q2 * merid) * weight, q0 * q3 * weight], axis=0))
        cols = pl.ds(at, LANE)
        term_cos[:, cols] = jnp.concatenate([terms[0] + terms[3], terms[1] + terms[2]], axis=0).astype(jnp.bfloat16)
        term_sin[:, cols] = jnp.concatenate([terms[0] - terms[3], terms[1] - terms[2]], axis=0).astype(jnp.bfloat16)

    keep_wave = jnp.where(active, 1.0, 0.0)
    real = jnp.dot(term_cos[...], cos_tab[...], preferred_element_type=jnp.float32)
    imag = jnp.dot(term_sin[...], sin_tab[...], preferred_element_type=jnp.float32)
    split = 2 * rows
    out_ref[0] = ((real[:split] + parity * real[split:]) * keep_wave).astype(out_ref.dtype)
    out_ref[1] = (-(imag[:split] + parity * imag[split:]) * keep_wave).astype(out_ref.dtype)

    flip = (
        lax.broadcasted_iota(jnp.int32, (LANE, LANE), 0) + lax.broadcasted_iota(jnp.int32, (LANE, LANE), 1) == LANE - 1
    ).astype(jnp.float32).astype(jnp.bfloat16)
    pad = jnp.zeros((rows, NPAD - width), jnp.float32)

    def reverse(image):
        parts = [
            jnp.dot(images[image, :, pl.ds(block * LANE, LANE)].astype(jnp.bfloat16), flip, preferred_element_type=jnp.float32)
            for block in reversed(range(blocks))
        ]
        return jnp.concatenate(parts + [pad], axis=1)

    def straight(image):
        return jnp.concatenate([images[image], pad], axis=1)

    halfway = row_points // 2
    total = straight(0)
    total = total + pltpu.roll(straight(1), halfway, axis=1)
    total = total + pltpu.roll(reverse(2), lax.rem(halfway - (width - 1) + NPAD, NPAD), axis=1)
    total = total + pltpu.roll(reverse(3), lax.rem(row_points - (width - 1) + NPAD, NPAD), axis=1)
    values_ref[...] = total.astype(values_ref.dtype)


def grid_stage(four, scales, row_points, assignment):
    _, rows, wave_count = four.shape
    width = -(-(wave_count + 5) // LANE) * LANE
    starts = -(-(width // LANE) // 8) * 8
    smem, vmem = pl.BlockSpec(memory_space=pltpu.SMEM), pl.BlockSpec(memory_space=pltpu.VMEM)
    f32, b16 = jnp.float32, jnp.bfloat16
    return pl.pallas_call(
        grid_kernel,
        out_shape=(jax.ShapeDtypeStruct((2, 2 * rows, wave_count), b16), jax.ShapeDtypeStruct((rows, NPAD), b16)),
        in_specs=[smem, vmem, vmem, vmem],
        out_specs=(vmem, vmem),
        scratch_shapes=[
            pltpu.VMEM((LANE, wave_count), f32),
            pltpu.VMEM((LANE, wave_count), f32),
            pltpu.VMEM((starts, wave_count), f32),
            pltpu.VMEM((starts, wave_count), f32),
            pltpu.VMEM((width, wave_count), b16),
            pltpu.VMEM((width, wave_count), b16),
            pltpu.VMEM((12 * rows, wave_count), b16),
            pltpu.VMEM((12 * rows, wave_count), b16),
            pltpu.VMEM((4 * rows, width), b16),
            pltpu.VMEM((4 * rows, width), b16),
            pltpu.VMEM((4, rows, width), f32),
        ],
        compiler_params=pltpu.CompilerParams(vmem_limit_bytes=40 * 1024 * 1024),
    )(row_points[None], scales, assignment[None, :], four)


def make_term(source, legendre):
    return jnp.einsum("knc,knt->ckt", source, legendre, preferred_element_type=jnp.float32)


def body(spectral, legendre, weights, points, assignment):
    own_slots, own_totals, column_count = spectral.shape
    wave_count = assignment.shape[0]
    levels = column_count // 8
    local_levels = levels // lax.axis_size("lev")
    own_waves = lax.dynamic_slice_in_dim(assignment, lax.axis_index("lat") * own_slots, own_slots)
    totals = lax.axis_index("lev") * own_totals + jnp.arange(own_totals, dtype=jnp.int32)
    triangle = totals[None, :] >= own_waves[:, None]
    masked = jnp.where(triangle[:, :, None], spectral, jnp.zeros((), spectral.dtype))
    summed = lax.psum_scatter(
        make_term(masked, legendre).astype(jnp.bfloat16), "lev", scatter_dimension=0, tiled=True
    )
    fourier = lax.all_to_all(summed, "lat", split_axis=2, concat_axis=1, tiled=True)
    pair_count = points.shape[0]
    grouped = fourier.reshape(local_levels, 2, 4, wave_count, pair_count, 2, 2)
    grouped = jnp.transpose(grouped, (4, 6, 1, 5, 0, 2, 3)).reshape(pair_count, 4, 8 * local_levels, wave_count)
    values, waves = [], []
    for pair in range(pair_count):
        scales = weights[2 * pair:2 * pair + 2] / points[pair].astype(jnp.float32)
        scales = jnp.repeat(scales, 4 * local_levels)[:, None]
        wave_rows, pair_values = grid_stage(grouped[pair], scales, points[pair], assignment)
        values.append(pair_values.reshape(2, local_levels, 4, NPAD))
        waves.append(wave_rows.reshape(2, 2, 2, local_levels, 4, wave_count))
    values = jnp.concatenate(values, axis=0)
    local_waves = jnp.transpose(jnp.stack(waves), (4, 1, 5, 6, 0, 3, 2))
    spread = lax.all_to_all(
        local_waves.reshape(8 * local_levels, wave_count, -1),
        "lat",
        split_axis=1,
        concat_axis=2,
        tiled=True,
    )
    result = jnp.einsum(
        "knt,ckt->knc",
        legendre,
        lax.all_gather(spread, "lev", axis=0, tiled=True),
        preferred_element_type=jnp.float32,
    )
    tendency = jnp.where(triangle[:, :, None], result, 0.0).astype(jnp.bfloat16)
    return (tendency, values)


def solution(mesh):
    in_specs = (P("lat", "lev", None), P("lat", "lev", None), P("lat"), P("lat"), P())
    out_specs = (P("lat", "lev", None), P("lat", "lev", None, None))
    return jax.shard_map(body, mesh=mesh, in_specs=in_specs, out_specs=out_specs, check_vma=False)
```

time: 594 us -> 121 us (0.20)
  other arithmetic: 431 us -> 0.11 us
  local copies, waits for them, and re-layouts: 30 us -> 12.4 us
  matrix products: 31.2 us -> 13.7 us
  loops' own time: 16.4 us -> 0 us
  Pallas kernels: 0 us -> 10.4 us
    convert_element_type x21 -> x0, other arithmetic: 398 us -> none  [block_table(): cosine_rows = jnp.where(active, cosine_vals, 0.0).astype(jnp.bfloat16)]
    lt x42 -> x0, other arithmetic: 27.4 us -> none  [the longest x21 13.7 us: block_table(): columns[None, :] < row_points]
    dot_general x42 -> x0, matrix products: 17.5 us -> none  [the longest x21 10.4 us: block_step(): lax.dot_general(terms.reshape(-1, XBLOCK), basis, (((1,), (1,)), ((), ())...]
    another operation x1 -> x0, loops' own time: 16.4 us -> none  [body(): lax.scan(block_step, start_sums, jnp.arange(block_count, dtype=jnp.int32))]
    dynamic_slice x21 -> x0, local copies, waits for them, and re-layouts: 12.3 us -> none  [body(): lax.scan(block_step, start_sums, jnp.arange(block_count, dtype=jnp.int32))]
    pallas_call x0 -> x1, Pallas kernels: none -> 10.4 us  [grid_stage(): pl.pallas_call(grid_kernel, out_shape=(jax.ShapeDtypeStruct((2, 2 * rows,...]
  transfers between devices with their start and end apart: 3 -> 3, of which waited for: 3 -> 3; matrix products, arithmetic and copies ran while one was open for 0% -> 1% of each run, Pallas kernels for 0% -> 0%
where the time goes in v1:
time: 121 us
  waiting for transfers between devices  42.7 us (35%)
  blocking collectives  17.7 us (15%)
  between operations  14.8 us (12%)
  matrix products  13.7 us (11%)
  local copies, waits for them, and re-layouts  12.4 us (10%)
  Pallas kernels  10.4 us (9%)
  starting transfers between devices  9.13 us (8%)
    reduce_scatter x1, waiting for transfers between devices, body(): lax.psum_scatter(make_term(masked, legendre).astype(jnp.bfloat16), 'lev',...  27.7 us
    all_gather x1, blocking collectives, body(): lax.all_gather(spread, 'lev', axis=0, tiled=True)  17.7 us
    pallas_call x1, Pallas kernels, grid_stage(): pl.pallas_call(grid_kernel, out_shape=(jax.ShapeDtypeStruct((2, 2 * rows,...  10.4 us
    all_to_all x1, waiting for transfers between devices, body(): lax.all_to_all(summed, 'lat', split_axis=2, concat_axis=1, tiled=True)  8.08 us
    dot_general x1, matrix products, make_term(): jnp.einsum('knc,knt->ckt', source, legendre, preferred_element_type=jnp.f...  7.2 us
    all_to_all x1, waiting for transfers between devices, body(): lax.all_to_all(local_waves.reshape(8 * local_levels, wave_count, -1), 'la...  6.85 us
    dot_general x1, matrix products, body(): jnp.einsum('knt,ckt->knc', legendre, lax.all_gather(spread, 'lev', axis=0...  6.52 us
    all_to_all x1, starting transfers between devices, body(): lax.all_to_all(summed, 'lat', split_axis=2, concat_axis=1, tiled=True)  5.5 us
  transfers between devices with their start and end apart: 3, of which 3 were waited for; matrix products, arithmetic and copies ran while one was open for 1% of the time, Pallas kernels for 0%

profile of v1, /device:TPU:0, one launch (start us, length us, event | category | flops | bytes accessed | tf_op | source)
XLA Modules:
  0.0 120.9 jit_solution(584570413888157412)
XLA Ops:
  7.2 0.0 reduce-scatter.2.cloned.1.call-start
  7.2 0.8 dynamic_slice.3
  8.0 0.1 broadcast_compare_fusion
  8.1 7.2 %fusion.8 = bf16[64,160,32]{0,2,1:T(8,128)(2,1)S(1)} fusion(bf16[160,320,32]{1,2,0:T(8,128)(2,1)} %param.6, bf16[160,320,64]{1,2,0:T(8,128)(2,1)} %param.5, pred[160,320]{1,0:T(8,128)(4,1)S(1)} %broadcast_compare_fusion), kind=kOutput, calls=%fused_computation.7 | convolution fusion | flops 213319680 | bytes 10536960 | tf_op jit(solution)/shard_map/knc,knt->ckt/dot_general | solution.py:182
  15.3 0.0 copy-start
  15.3 0.0 copy-start.1
  15.3 3.0 %copy.14 = bf16[64,160,32]{1,2,0:T(8,128)(2,1)} copy(bf16[64,160,32]{0,2,1:T(8,128)(2,1)S(1)} %fusion.8) | data formatting | bytes 1310720 | tf_op jit(solution)/shard_map/convert_element_type | solution.py:195
  18.3 0.0 reduce-scatter.2.cloned.1.call-update
  18.3 27.7 %reduce-scatter.2.cloned.1.call-done = bf16[16,160,32]{1,2,0:T(8,128)(2,1)} async-done(((bf16[64,160,32]{1,2,0:T(8,128)(2,1)}), bf16[16,160,32]{1,2,0:T(8,128)(2,1)}) %reduce-scatter.2.cloned.1.call-update) | async-done | bytes 163856 | tf_op jit(solution)/shard_map/reduce_scatter | solution.py:194
  46.1 1.8 %copy.15 = bf16[16,160,32]{1,0,2:T(8,128)(2,1)} copy(bf16[16,160,32]{1,2,0:T(8,128)(2,1)} %reduce-scatter.2.cloned.1.call-done) | data formatting | bytes 327680 | tf_op jit(solution)/shard_map/reduce_scatter | solution.py:194
  47.9 5.5 %all-to-all-start = ((bf16[16,160,32]{1,0,2:T(8,128)(2,1)}), bf16[16,160,32]{1,0,2:T(8,128)(2,1)S(1)}, u32[]{:S(2)}, u32[]{:S(2)}) async-start(bf16[16,160,32]{1,0,2:T(8,128)(2,1)} %copy.15), calls=%async_computation.1 | async-start | bytes 524288 | tf_op jit(solution)/shard_map/all_to_all | solution.py:197
  53.4 0.0 copy-done
  54.0 0.0 copy-done.1
  54.1 0.1 broadcast_in_dim.35
  54.1 0.1 broadcast_in_dim_reshape.4.scales_ref
  54.2 8.1 %all-to-all-done = bf16[16,160,32]{1,0,2:T(8,128)(2,1)S(1)} async-done(((bf16[16,160,32]{1,0,2:T(8,128)(2,1)}), bf16[16,160,32]{1,0,2:T(8,128)(2,1)S(1)}, u32[]{:S(2)}, u32[]{:S(2)}) %all-to-all-start) | async-done | bytes 163872 | tf_op jit(solution)/shard_map/all_to_all | solution.py:197
  62.3 0.1 copy.28
  62.4 0.4 reshape.47
  62.8 0.1 copy.17
  63.0 10.4 %shard_map.68 = (bf16[2,32,1280]{2,1,0:T(8,128)(2,1)S(1)}, bf16[16,5376]{1,0:T(8,128)(2,1)S(1)}) custom-call(s32[1]{0:T(128)S(6)} %copy.30.points_ref, f32[16,1]{1,0:T(8,128)S(1)} %broadcast_in_dim_reshape.4.scales_ref, s32[1,1280]{1,0:T(1,128)S(1)} %broadcast_in_dim.36.waves_ref, bf16[4,16,1280]{2,1,0:T(8,128)(2,1)S(1)} %squeeze_reshape.3.four_ref), custom_call_target="tpu_custom_call" | custom-call | tf_op jit(solution)/shard_map/pallas_call | solution.py:159
  73.4 0.1 copy.29
  73.5 0.8 copy.20
  74.3 2.1 %reshape.50 = bf16[8,2,5120]{2,1,0:T(2,128)(2,1)} reshape(bf16[1280,4,16]{2,1,0:T(4,128)(2,1)S(1)} %bitcast.29) | data formatting | bytes 327680
  76.3 3.6 %all-to-all-start.1 = ((bf16[8,2,5120]{2,1,0:T(2,128)(2,1)}), bf16[8,2,5120]{2,1,0:T(2,128)(2,1)S(1)}, u32[]{:S(2)}, u32[]{:S(2)}) async-start(bf16[8,2,5120]{2,1,0:T(2,128)(2,1)} %reshape.50), calls=%async_computation.2 | async-start | bytes 327680 | tf_op jit(solution)/shard_map/all_to_all | solution.py:210
  79.9 0.7 reshape.49
  80.7 6.8 %all-to-all-done.1 = bf16[8,2,5120]{2,1,0:T(2,128)(2,1)S(1)} async-done(((bf16[8,2,5120]{2,1,0:T(2,128)(2,1)}), bf16[8,2,5120]{2,1,0:T(2,128)(2,1)S(1)}, u32[]{:S(2)}, u32[]{:S(2)}) %all-to-all-start.1) | async-done | bytes 163872 | tf_op jit(solution)/shard_map/all_to_all | solution.py:210
  87.5 0.9 reshape.51
  88.4 0.7 copy.25
  89.2 0.7 copy.23
  89.9 17.7 %all_gather.3 = bf16[64,160,32]{2,0,1:T(8,128)(2,1)S(1)} all-gather(bf16[16,160,32]{2,0,1:T(8,128)(2,1)S(1)} %copy.23), channel_id=1, replica_groups=mesh['lat'=8,'lev'=4] {'lev'}, dimensions={0}, use_global_device_ids=true | all-gather | bytes 819200 | tf_op jit(solution)/shard_map/all_gather | solution.py:220
  107.5 6.5 %fusion.3 = bf16[160,320,64]{1,2,0:T(8,128)(2,1)} fusion(bf16[64,160,32]{2,0,1:T(8,128)(2,1)S(1)} %all_gather.3, bf16[160,320,32]{1,2,0:T(8,128)(2,1)} %param.6, pred[160,320]{1,0:T(8,128)(4,1)S(1)} %broadcast_compare_fusion), kind=kOutput, calls=%fused_computation.4 | convolution fusion | flops 216268800 | bytes 10536960 | tf_op jit(solution)/shard_map/knt,ckt->knc/dot_general | solution.py:217
  (6 shorter events, 0.1 us)
Async XLA Ops:
  7.2 38.9 %reduce-scatter.2.cloned.1.call-start = ((), (), s32[]{:S(2)}) async-start(), calls=%async_computation.3 | async-start | bytes 1310720 | tf_op jit(solution)/shard_map/reduce_scatter | solution.py:194
  15.3 38.1 %copy-start = (s32[1280]{0:T(1024)S(1)}, s32[1280]{0:T(1024)}, u32[]{:S(2)}) copy-start(s32[1280]{0:T(1024)} %param.9) | copy-start | bytes 15364
  15.3 38.7 %copy-start.1 = (f32[2]{0:T(128)S(1)}, f32[2]{0:T(128)}, u32[]{:S(2)}) copy-start(f32[2]{0:T(128)} %param.7) | copy-start | bytes 28
  47.9 14.4 %all-to-all-start = ((bf16[16,160,32]{1,0,2:T(8,128)(2,1)}), bf16[16,160,32]{1,0,2:T(8,128)(2,1)S(1)}, u32[]{:S(2)}, u32[]{:S(2)}) async-start(bf16[16,160,32]{1,0,2:T(8,128)(2,1)} %copy.15), calls=%async_computation.1 | async-start | bytes 524288 | tf_op jit(solution)/shard_map/all_to_all | solution.py:197
  76.3 11.2 %all-to-all-start.1 = ((bf16[8,2,5120]{2,1,0:T(2,128)(2,1)}), bf16[8,2,5120]{2,1,0:T(2,128)(2,1)S(1)}, u32[]{:S(2)}, u32[]{:S(2)}) async-start(bf16[8,2,5120]{2,1,0:T(2,128)(2,1)} %reshape.50), calls=%async_computation.2 | async-start | bytes 327680 | tf_op jit(solution)/shard_map/all_to_all | solution.py:210
Sparse Core Ops, SparseCore 0:
  18.4 27.5 reduce-scatter.1

commit v2 on v1

--- a/solution.py
+++ b/solution.py
@@ -1,3 +1,4 @@
+import functools
 import math
 
 import jax
@@ -81,8 +82,13 @@
     parity = jnp.where((m_int & 1) == 0, 1.0, -1.0)
     factor = jnp.where(active, jnp.where(m_int == 0, 1.0, 2.0), 0.0)
     slope = factor * (m_float * (1.0 / wave_count))
-    real_value, imag_value = four_ref[0].astype(jnp.float32), four_ref[1].astype(jnp.float32)
-    real_slope, imag_slope = four_ref[2].astype(jnp.float32), four_ref[3].astype(jnp.float32)
+    part_rows = rows // 2
+
+    def rows_of(slope_of, part):
+        pieces = [four_ref[2 * row + slope_of].astype(jnp.float32) for row in range(2)]
+        return jnp.concatenate([piece[part * part_rows:(part + 1) * part_rows] for piece in pieces], axis=0)
+
+    real_value, imag_value, real_slope, imag_slope = rows_of(0, 0), rows_of(0, 1), rows_of(1, 0), rows_of(1, 1)
 
     def fill(lhs, value, zonal, merid):
         parts = [value, shift_field(value, 1), shift_field(value, 2), shift_field(value, 3), zonal, merid]
@@ -124,8 +130,13 @@
     real = jnp.dot(term_cos[...], cos_tab[...], preferred_element_type=jnp.float32)
     imag = jnp.dot(term_sin[...], sin_tab[...], preferred_element_type=jnp.float32)
     split = 2 * rows
-    out_ref[0] = ((real[:split] + parity * real[split:]) * keep_wave).astype(out_ref.dtype)
-    out_ref[1] = (-(imag[:split] + parity * imag[split:]) * keep_wave).astype(out_ref.dtype)
+    real = (real[:split] + parity * real[split:]) * keep_wave
+    imag = -(imag[:split] + parity * imag[split:]) * keep_wave
+    for term in range(2):
+        for row in range(2):
+            low = term * rows + row * part_rows
+            both = [real[low:low + part_rows], imag[low:low + part_rows]]
+            out_ref[2 * row + term] = jnp.concatenate(both, axis=0).astype(out_ref.dtype)
 
     flip = (
         lax.broadcasted_iota(jnp.int32, (LANE, LANE), 0) + lax.broadcasted_iota(jnp.int32, (LANE, LANE), 1) == LANE - 1
@@ -158,7 +169,7 @@
     f32, b16 = jnp.float32, jnp.bfloat16
     return pl.pallas_call(
         grid_kernel,
-        out_shape=(jax.ShapeDtypeStruct((2, 2 * rows, wave_count), b16), jax.ShapeDtypeStruct((rows, NPAD), b16)),
+        out_shape=(jax.ShapeDtypeStruct((4, rows, wave_count), b16), jax.ShapeDtypeStruct((rows, NPAD), b16)),
         in_specs=[smem, vmem, vmem, vmem],
         out_specs=(vmem, vmem),
         scratch_shapes=[
@@ -178,49 +189,255 @@
     )(row_points[None], scales, assignment[None, :], four)
 
 
-def make_term(source, legendre):
-    return jnp.einsum("knc,knt->ckt", source, legendre, preferred_element_type=jnp.float32)
+def split_column(column):
+    return (column // 4 % 2) * 8 + column // 8 * 4 + column % 4
+
+
+def greet(lat_size, lev_size):
+    lat, lev = lax.axis_index("lat"), lax.axis_index("lev")
+    barrier = pltpu.get_barrier_semaphore()
+    for hop in range(1, lev_size):
+        pl.semaphore_signal(barrier, inc=1, device_id=(lat, lax.rem(lev + hop, lev_size)), device_id_type=pl.DeviceIdType.MESH)
+    for hop in range(1, lat_size):
+        pl.semaphore_signal(barrier, inc=1, device_id=(lax.rem(lat + hop, lat_size), lev), device_id_type=pl.DeviceIdType.MESH)
+    pl.semaphore_wait(barrier, lat_size + lev_size - 2)
+
+
+def remote(src, dst, send_sem, recv_sem, device):
+    return pltpu.make_async_remote_copy(
+        src_ref=src, dst_ref=dst, send_sem=send_sem, recv_sem=recv_sem,
+        device_id=device, device_id_type=pl.DeviceIdType.MESH,
+    )
+
+
+def inverse_kernel(
+    lat_size, lev_size, pack, chunks,
+    own_ref, spec_hbm, leg_hbm, out_ref,
+    spec, leg, lev_send, lev_recv, summed, turned, lat_send, lat_recv,
+    load_sem, lev_send_sem, lev_recv_sem, lat_send_sem, lat_recv_sem,
+):
+    lat, lev = lax.axis_index("lat"), lax.axis_index("lev")
+    _, groups, columns, totals = spec.shape
+    rows = leg.shape[2]
+    size = groups // chunks
+    loads = []
+    for chunk in range(chunks):
+        part = pl.ds(chunk * size, size)
+        pair = [
+            pltpu.make_async_copy(spec_hbm.at[:, part], spec.at[:, part], load_sem.at[chunk, 0]),
+            pltpu.make_async_copy(leg_hbm.at[:, part], leg.at[:, part], load_sem.at[chunk, 1]),
+        ]
+        for copy in pair:
+            copy.start()
+        loads.append(pair)
+    greet(lat_size, lev_size)
+    number = lax.broadcasted_iota(jnp.int32, (1, totals), 1) + lev * totals
+    lane = lax.broadcasted_iota(jnp.int32, (1, pack * rows), 1) // rows
+    share = columns // lev_size
+    copies = []
+    for chunk in range(chunks):
+        for copy in loads[chunk]:
+            copy.wait()
+
+        @pl.loop(chunk * size, (chunk + 1) * size)
+        def _(group):
+            tables = []
+            for which in range(pack):
+                kept = jnp.where(number >= own_ref[which * groups + group], 1.0, 0.0).astype(jnp.bfloat16)
+                tables.append(leg[which, group] * kept)
+            table = jnp.concatenate(tables, axis=0)
+            source = jnp.concatenate([spec[which, group] for which in range(pack)], axis=0)
+            product = lax.dot_general(source, table, (((1,), (1,)), ((), ())), preferred_element_type=jnp.float32)
+            result = product[:columns]
+            for which in range(1, pack):
+                result = jnp.where(lane == which, product[which * columns:(which + 1) * columns], result)
+            result = result.astype(jnp.bfloat16)
+            for peer in range(lev_size):
+                lev_send[peer, group] = result[peer * share:(peer + 1) * share]
+
+        part = pl.ds(chunk * size, size)
+        for hop in range(1, lev_size):
+            peer = lax.rem(lev + hop, lev_size)
+            copy = remote(
+                lev_send.at[peer, part], lev_recv.at[hop - 1, part],
+                lev_send_sem.at[chunk, hop - 1], lev_recv_sem.at[chunk, hop - 1], (lat, peer),
+            )
+            copy.start()
+            copies.append(copy)
+    for chunk in range(chunks):
+        for hop in range(1, lev_size):
+            copies[chunk * (lev_size - 1) + hop - 1].wait_recv()
+        part = pl.ds(chunk * size, size)
+        total = lev_send[lev, part].astype(jnp.float32)
+        for hop in range(1, lev_size):
+            total = total + lev_recv[hop - 1, part].astype(jnp.float32)
+        summed[part] = total
+    for column in range(share):
+        flat = jnp.transpose(summed[:, column, :])
+        turned[:, split_column(column), :] = jnp.concatenate(
+            [flat[which * rows:(which + 1) * rows] for which in range(pack)], axis=1
+        )
+    lat_send[...] = turned[...].astype(jnp.bfloat16)
+    block = rows // lat_size
+    swaps = []
+    for hop in range(1, lat_size):
+        peer = lax.rem(lat + hop, lat_size)
+        copy = remote(
+            lat_send.at[pl.ds(peer * block, block)], lat_recv.at[lat],
+            lat_send_sem.at[hop - 1], lat_recv_sem.at[hop - 1], (peer, lev),
+        )
+        copy.start()
+        swaps.append(copy)
+    lat_recv[lat] = lat_send[pl.ds(lat * block, block)]
+    for copy in copies:
+        copy.wait_send()
+    for copy in swaps:
+        copy.wait()
+    for row in range(block):
+        pieces = [lat_recv[source, row].astype(jnp.float32) for source in range(lat_size)]
+        out_ref[row] = jnp.concatenate(pieces, axis=1).astype(jnp.bfloat16)
+
+
+def direct_kernel(
+    lat_size, lev_size, pack,
+    waves_ref, out_ref,
+    lat_send, lat_recv, turned, grouped, lev_send, lev_recv,
+    lat_send_sem, lat_recv_sem, lev_send_sem, lev_recv_sem,
+):
+    lat, lev = lax.axis_index("lat"), lax.axis_index("lev")
+    block, share, _ = waves_ref.shape
+    own = lat_send.shape[3]
+    rows, groups = lat_size * block, own // pack
+    for row in range(block):
+        line = waves_ref[row].astype(jnp.float32)
+        for peer in range(lat_size):
+            lat_send[peer, row] = line[:, peer * own:(peer + 1) * own].astype(jnp.bfloat16)
+    greet(lat_size, lev_size)
+    swaps = []
+    for hop in range(1, lat_size):
+        peer = lax.rem(lat + hop, lat_size)
+        copy = remote(lat_send.at[peer], lat_recv.at[lat], lat_send_sem.at[hop - 1], lat_recv_sem.at[hop - 1], (peer, lev))
+        copy.start()
+        swaps.append(copy)
+    lat_recv[lat] = lat_send[lat]
+    for copy in swaps:
+        copy.wait()
+    turned[...] = lat_recv[...].astype(jnp.float32).reshape(rows, share, own)
+    for column in range(share):
+        line = turned[:, split_column(column), :]
+        flat = jnp.concatenate([line[:, which * groups:(which + 1) * groups] for which in range(pack)], axis=0)
+        grouped[:, column, :] = jnp.transpose(flat)
+    lev_send[...] = grouped[...].astype(jnp.bfloat16)
+    copies = []
+    for hop in range(1, lev_size):
+        peer = lax.rem(lev + hop, lev_size)
+        copy = remote(lev_send, lev_recv.at[lev], lev_send_sem.at[hop - 1], lev_recv_sem.at[hop - 1], (lat, peer))
+        copy.start()
+        copies.append(copy)
+    lev_recv[lev] = lev_send[...]
+    for copy in copies:
+        copy.wait()
+    out_ref[...] = lev_recv[...]
+
+
+def tendency_kernel(own_ref, waves_ref, leg_ref, out_ref):
+    pack, size, rows, totals = leg_ref.shape
+    groups = size * pl.num_programs(0)
+    lev_size, _, share, lanes = waves_ref.shape
+    columns = lev_size * share
+    first = pl.program_id(0) * size
+    number = lax.broadcasted_iota(jnp.int32, (1, totals), 1) + lax.axis_index("lev") * totals
+    lane = lax.broadcasted_iota(jnp.int32, (1, lanes), 1) // rows
+
+    @pl.loop(0, size)
+    def _(group):
+        waves = jnp.concatenate([waves_ref[peer, group] for peer in range(lev_size)], axis=0)
+        spread = jnp.concatenate(
+            [waves * jnp.where(lane == which, 1.0, 0.0).astype(jnp.bfloat16) for which in range(pack)], axis=0
+        )
+        table = jnp.concatenate([leg_ref[which, group] for which in range(pack)], axis=0)
+        product = jnp.dot(spread, table, preferred_element_type=jnp.float32)
+        for which in range(pack):
+            kept = number >= own_ref[which * groups + first + group]
+            out_ref[which, group] = jnp.where(kept, product[which * columns:(which + 1) * columns], 0.0).astype(jnp.bfloat16)
 
 
 def body(spectral, legendre, weights, points, assignment):
     own_slots, own_totals, column_count = spectral.shape
     wave_count = assignment.shape[0]
+    rows = legendre.shape[2]
     levels = column_count // 8
-    local_levels = levels // lax.axis_size("lev")
+    lat_size, lev_size = lax.axis_size("lat"), lax.axis_size("lev")
+    local_levels = levels // lev_size
+    share = column_count // lev_size
+    pack = LANE // rows
+    groups = own_slots // pack
+    block = rows // lat_size
+    chunks = 5
     own_waves = lax.dynamic_slice_in_dim(assignment, lax.axis_index("lat") * own_slots, own_slots)
-    totals = lax.axis_index("lev") * own_totals + jnp.arange(own_totals, dtype=jnp.int32)
-    triangle = totals[None, :] >= own_waves[:, None]
-    masked = jnp.where(triangle[:, :, None], spectral, jnp.zeros((), spectral.dtype))
-    summed = lax.psum_scatter(
-        make_term(masked, legendre).astype(jnp.bfloat16), "lev", scatter_dimension=0, tiled=True
-    )
-    fourier = lax.all_to_all(summed, "lat", split_axis=2, concat_axis=1, tiled=True)
-    pair_count = points.shape[0]
-    grouped = fourier.reshape(local_levels, 2, 4, wave_count, pair_count, 2, 2)
-    grouped = jnp.transpose(grouped, (4, 6, 1, 5, 0, 2, 3)).reshape(pair_count, 4, 8 * local_levels, wave_count)
-    values, waves = [], []
-    for pair in range(pair_count):
-        scales = weights[2 * pair:2 * pair + 2] / points[pair].astype(jnp.float32)
-        scales = jnp.repeat(scales, 4 * local_levels)[:, None]
-        wave_rows, pair_values = grid_stage(grouped[pair], scales, points[pair], assignment)
-        values.append(pair_values.reshape(2, local_levels, 4, NPAD))
-        waves.append(wave_rows.reshape(2, 2, 2, local_levels, 4, wave_count))
-    values = jnp.concatenate(values, axis=0)
-    local_waves = jnp.transpose(jnp.stack(waves), (4, 1, 5, 6, 0, 3, 2))
-    spread = lax.all_to_all(
-        local_waves.reshape(8 * local_levels, wave_count, -1),
-        "lat",
-        split_axis=1,
-        concat_axis=2,
-        tiled=True,
-    )
-    result = jnp.einsum(
-        "knt,ckt->knc",
-        legendre,
-        lax.all_gather(spread, "lev", axis=0, tiled=True),
-        preferred_element_type=jnp.float32,
-    )
-    tendency = jnp.where(triangle[:, :, None], result, 0.0).astype(jnp.bfloat16)
+    spec_in = jnp.transpose(spectral, (0, 2, 1)).reshape(pack, groups, column_count, own_totals)
+    leg_in = jnp.transpose(legendre, (0, 2, 1)).reshape(pack, groups, rows, own_totals)
+    smem, vmem = pl.BlockSpec(memory_space=pltpu.SMEM), pl.BlockSpec(memory_space=pltpu.VMEM)
+    anywhere = pl.BlockSpec(memory_space=pl.ANY)
+    f32, b16 = jnp.float32, jnp.bfloat16
+    dma = pltpu.SemaphoreType.DMA
+    fourier = pl.pallas_call(
+        functools.partial(inverse_kernel, lat_size, lev_size, pack, chunks),
+        out_shape=jax.ShapeDtypeStruct((block, share, wave_count), b16),
+        in_specs=[smem, anywhere, anywhere],
+        out_specs=vmem,
+        scratch_shapes=[
+            pltpu.VMEM((pack, groups, column_count, own_totals), b16),
+            pltpu.VMEM((pack, groups, rows, own_totals), b16),
+            pltpu.VMEM((lev_size, groups, share, pack * rows), b16),
+            pltpu.VMEM((lev_size - 1, groups, share, pack * rows), b16),
+            pltpu.VMEM((groups, share, pack * rows), f32),
+            pltpu.VMEM((rows, share, own_slots), f32),
+            pltpu.VMEM((rows, share, own_slots), b16),
+            pltpu.VMEM((lat_size, block, share, own_slots), b16),
+            dma((chunks, 2)), dma((chunks, lev_size - 1)), dma((chunks, lev_size - 1)),
+            dma((lat_size - 1,)), dma((lat_size - 1,)),
+        ],
+        compiler_params=pltpu.CompilerParams(
+            collective_id=0, has_side_effects=True, vmem_limit_bytes=40 * 1024 * 1024
+        ),
+    )(own_waves, spec_in, leg_in)
+    scales = weights / points[0].astype(jnp.float32)
+    scales = jnp.repeat(scales, 4 * local_levels)[:, None]
+    wave_rows, values = grid_stage(fourier, scales, points[0], assignment)
+    values = values.reshape(2, local_levels, 4, NPAD)
+    gathered = pl.pallas_call(
+        functools.partial(direct_kernel, lat_size, lev_size, pack),
+        out_shape=jax.ShapeDtypeStruct((lev_size, groups, share, pack * rows), b16),
+        in_specs=[vmem],
+        out_specs=vmem,
+        scratch_shapes=[
+            pltpu.VMEM((lat_size, block, share, own_slots), b16),
+            pltpu.VMEM((lat_size, block, share, own_slots), b16),
+            pltpu.VMEM((rows, share, own_slots), f32),
+            pltpu.VMEM((groups, share, pack * rows), f32),
+            pltpu.VMEM((groups, share, pack * rows), b16),
+            pltpu.VMEM((lev_size, groups, share, pack * rows), b16),
+            dma((lat_size - 1,)), dma((lat_size - 1,)), dma((lev_size - 1,)), dma((lev_size - 1,)),
+        ],
+        compiler_params=pltpu.CompilerParams(
+            collective_id=1, has_side_effects=True, vmem_limit_bytes=40 * 1024 * 1024
+        ),
+    )(wave_rows)
+    size = groups // 5
+    result = pl.pallas_call(
+        tendency_kernel,
+        grid=(groups // size,),
+        out_shape=jax.ShapeDtypeStruct((pack, groups, column_count, own_totals), b16),
+        in_specs=[
+            smem,
+            pl.BlockSpec((lev_size, size, share, pack * rows), lambda step: (0, step, 0, 0)),
+            pl.BlockSpec((pack, size, rows, own_totals), lambda step: (0, step, 0, 0)),
+        ],
+        out_specs=pl.BlockSpec((pack, size, column_count, own_totals), lambda step: (0, step, 0, 0)),
+        compiler_params=pltpu.CompilerParams(vmem_limit_bytes=40 * 1024 * 1024),
+    )(own_waves, gathered, leg_in)
+    tendency = jnp.transpose(result.reshape(own_slots, column_count, own_totals), (0, 2, 1))
     return (tendency, values)
 
 

time: 121 us -> 76.4 us (0.63); the launches traced: 121 us -> 74.9 us
  Pallas kernels: 10.4 us -> 63.1 us
  waiting for transfers between devices: 42.7 us -> 0 us
  blocking collectives: 17.7 us -> 0 us
  matrix products: 13.7 us -> 0 us
  between operations: 14.8 us -> 1.32 us
  starting transfers between devices: 9.13 us -> 0 us
  local copies, waits for them, and re-layouts: 12.4 us -> 9.79 us
    pallas_call x1 -> x4, Pallas kernels: 10.4 us -> 63.1 us  [the longest x1 26.8 us: body(): pl.pallas_call(functools.partial(inverse_kernel, lat_size, lev_size, pack...]
    reduce_scatter x1 -> x0, waiting for transfers between devices: 27.7 us -> none  [body(): lax.psum_scatter(make_term(masked, legendre).astype(jnp.bfloat16), 'lev',...]
    all_gather x1 -> x0, blocking collectives: 17.7 us -> none  [body(): lax.all_gather(spread, 'lev', axis=0, tiled=True)]
    all_to_all x2 -> x0, waiting for transfers between devices: 14.9 us -> none  [the longest x1 8.08 us: body(): lax.all_to_all(summed, 'lat', split_axis=2, concat_axis=1, tiled=True)]
    dot_general x2 -> x0, matrix products: 13.7 us -> none  [the longest x1 7.2 us: make_term(): jnp.einsum('knc,knt->ckt', source, legendre, preferred_element_type=jnp.f...]
    all_to_all x2 -> x0, starting transfers between devices: 9.09 us -> none  [the longest x1 5.5 us: body(): lax.all_to_all(summed, 'lat', split_axis=2, concat_axis=1, tiled=True)]
    unnamed x6, local copies, waits for them, and re-layouts: 2.99 us -> 7.46 us
    convert_element_type x1 -> x0, local copies, waits for them, and re-layouts: 2.96 us -> none  [body(): make_term(masked, legendre).astype(jnp.bfloat16)]
  transfers between devices with their start and end apart: 3 -> 0, of which waited for: 3 -> 0; matrix products, arithmetic and copies ran while one was open for 1% -> 0% of each run, Pallas kernels for 0% -> 0%
where the time goes in v2:
time: 76.4 us; the launch traced here: 74.9 us
  Pallas kernels  63.1 us (83%)
  local copies, waits for them, and re-layouts  9.79 us (13%)
  between operations  1.32 us (2%)
    pallas_call x1, Pallas kernels, body(): pl.pallas_call(functools.partial(inverse_kernel, lat_size, lev_size, pack...  26.8 us
    pallas_call x1, Pallas kernels, body(): pl.pallas_call(functools.partial(direct_kernel, lat_size, lev_size, pack)...  15.8 us
    pallas_call x1, Pallas kernels, grid_stage(): pl.pallas_call(grid_kernel, out_shape=(jax.ShapeDtypeStruct((4, rows, wav...  10.3 us
    pallas_call x1, Pallas kernels, body(): pl.pallas_call(tendency_kernel, grid=(groups // size,), out_shape=jax.Sha...  10.1 us
    unnamed x6, local copies, waits for them, and re-layouts  7.46 us

profile of v2, /device:TPU:0, one launch (start us, length us, event | category | flops | bytes accessed | tf_op | source)
XLA Modules:
  0.0 74.9 jit_solution(7617771586575496462)
XLA Ops:
  1.3 0.7 broadcast_divide_fusion
  1.9 0.8 %dynamic_slice.3.own_ref = s32[160]{0:T(256)S(1)} dynamic-slice(s32[1280]{0:T(1024)} %param.9, s32[]{:T(128)S(6)} %select_n.3), dynamic_slice_sizes={160} | dynamic-slice | bytes 1284 | tf_op jit(solution)/shard_map/dynamic_slice | solution.py:377
  2.7 0.1 broadcast_in_dim.6
  2.8 0.7 broadcast_in_dim.7.waves_ref
  3.5 0.1 broadcast_in_dim_reshape.4.scales_ref
  3.6 0.0 copy-start
  3.6 2.1 %copy-done = bf16[160,320,32]{1,2,0:T(8,128)(2,1)S(1)} copy-done((bf16[160,320,32]{1,2,0:T(8,128)(2,1)S(1)}, bf16[160,320,32]{1,2,0:T(8,128)(2,1)}, u32[]{:S(2)}) %copy-start) | copy-done | bytes 3276824
  5.7 0.0 copy-start.2
  5.7 3.2 %copy-done.2 = bf16[160,320,64]{1,2,0:T(8,128)(2,1)S(1)} copy-done((bf16[160,320,64]{1,2,0:T(8,128)(2,1)S(1)}, bf16[160,320,64]{1,2,0:T(8,128)(2,1)}, u32[]{:S(2)}) %copy-start.2) | copy-done | bytes 6553624
  8.9 26.8 %shard_map.68.four_ref = bf16[4,16,1280]{2,1,0:T(8,128)(2,1)S(1)} custom-call(s32[160]{0:T(256)S(1)} %dynamic_slice.3.own_ref, bf16[4,40,64,320]{3,2,1,0:T(8,128)(2,1)S(1)} %bitcast.12, bf16[4,40,32,320]{3,2,1,0:T(8,128)(2,1)S(1)} %bitcast.10), custom_call_target="tpu_custom_call" | custom-call | tf_op jit(solution)/shard_map/pallas_call | solution.py:384
  35.8 10.3 %shard_map.69 = (bf16[4,16,1280]{2,1,0:T(8,128)(2,1)S(1)}, bf16[16,5376]{1,0:T(8,128)(2,1)S(1)}) custom-call(s32[1]{0:T(128)S(6)} %copy.8.points_ref, f32[16,1]{1,0:T(8,128)S(1)} %broadcast_in_dim_reshape.4.scales_ref, s32[1,1280]{1,0:T(1,128)S(1)} %broadcast_in_dim.7.waves_ref, bf16[4,16,1280]{2,1,0:T(8,128)(2,1)S(1)} %shard_map.68.four_ref), custom_call_target="tpu_custom_call" | custom-call | tf_op jit(solution)/shard_map/pallas_call | solution.py:170
  46.1 0.7 reshape.20
  46.8 15.8 %shard_map.70.waves_ref = bf16[4,40,16,128]{3,2,1,0:T(8,128)(2,1)S(1)} custom-call(bf16[4,16,1280]{2,1,0:T(8,128)(2,1)S(1)} %get-tuple-element.4.waves_ref), custom_call_target="tpu_custom_call" | custom-call | tf_op jit(solution)/shard_map/pallas_call | solution.py:409
  62.6 0.0 copy-start.1
  62.6 2.1 %copy-done.1 = bf16[160,320,32]{1,2,0:T(8,128)(2,1)S(1)} copy-done((bf16[160,320,32]{1,2,0:T(8,128)(2,1)S(1)}, bf16[160,320,32]{1,2,0:T(8,128)(2,1)}, u32[]{:S(2)}) %copy-start.1) | copy-done | bytes 3276824
  64.7 10.1 %shard_map.71 = bf16[4,40,64,320]{3,2,1,0:T(8,128)(2,1)} custom-call(s32[160]{0:T(256)S(1)} %dynamic_slice.3.own_ref, bf16[4,40,16,128]{3,2,1,0:T(8,128)(2,1)S(1)} %shard_map.70.waves_ref, bf16[4,40,32,320]{3,2,1,0:T(8,128)(2,1)S(1)} %bitcast.11), custom_call_target="tpu_custom_call" | custom-call | tf_op jit(solution)/shard_map/pallas_call | solution.py:428
Async XLA Ops:
  3.6 2.1 %copy-start = (bf16[160,320,32]{1,2,0:T(8,128)(2,1)S(1)}, bf16[160,320,32]{1,2,0:T(8,128)(2,1)}, u32[]{:S(2)}) copy-start(bf16[160,320,32]{1,2,0:T(8,128)(2,1)} %param.6) | copy-start | bytes 9830404
  5.7 3.2 %copy-start.2 = (bf16[160,320,64]{1,2,0:T(8,128)(2,1)S(1)}, bf16[160,320,64]{1,2,0:T(8,128)(2,1)}, u32[]{:S(2)}) copy-start(bf16[160,320,64]{1,2,0:T(8,128)(2,1)} %param.5) | copy-start | bytes 19660804
  62.6 2.1 %copy-start.1 = (bf16[160,320,32]{1,2,0:T(8,128)(2,1)S(1)}, bf16[160,320,32]{1,2,0:T(8,128)(2,1)}, u32[]{:S(2)}) copy-start(bf16[160,320,32]{1,2,0:T(8,128)(2,1)} %param.6) | copy-start | bytes 9830404

commit v3 on v2

--- a/solution.py
+++ b/solution.py
@@ -38,14 +38,9 @@
     )
 
 
-def grid_kernel(
-    points_ref, scales_ref, waves_ref, four_ref, out_ref, values_ref,
-    base_cos, base_sin, start_cos, start_sin, cos_tab, sin_tab, lhs_cos, lhs_sin, term_cos, term_sin, images,
-):
+def build_tables(points_ref, waves_ref, base_cos, base_sin, start_cos, start_sin, cos_tab, sin_tab):
     width = cos_tab.shape[0]
     wave_count = cos_tab.shape[1]
-    rows = four_ref.shape[1]
-    blocks = width // LANE
     row_points = points_ref[0]
     quarter_int = row_points // 4
     quarter = quarter_int.astype(jnp.float32)
@@ -58,13 +53,13 @@
 
     start_cos[...], start_sin[...] = sincos(start_rows(start_cos.shape[0], LANE) * m_float, quarter, step)
 
-    @pl.loop(0, LANE // 8)
+    @pl.loop(0, LANE // 8, unroll=2)
     def _(index):
         at = pl.multiple_of(index * 8, 8)
         offsets = (lax.broadcasted_iota(jnp.int32, (8, 1), 0) + at).astype(jnp.float32)
         base_cos[pl.ds(at, 8), :], base_sin[pl.ds(at, 8), :] = sincos(offsets * m_float, quarter, step)
 
-    @pl.loop(0, width // 16)
+    @pl.loop(0, width // 16, unroll=2)
     def _(index):
         at = pl.multiple_of(index * 16, 16)
         low = pl.multiple_of((index % (LANE // 16)) * 16, 16)
@@ -78,6 +73,18 @@
             cos_tab[pl.ds(at, 16), cols] = (sc * bc - ss * bs).astype(jnp.bfloat16)
             sin_tab[pl.ds(at, 16), cols] = (ss * bc + sc * bs).astype(jnp.bfloat16)
 
+
+def grid_rows(
+    points_ref, scales_ref, waves_ref, four_ref, out_ref,
+    cos_tab, sin_tab, lhs_cos, lhs_sin, term_cos, term_sin, images,
+):
+    width, wave_count = cos_tab.shape
+    rows = four_ref.shape[1]
+    blocks = width // LANE
+    row_points = points_ref[0]
+    quarter_int = row_points // 4
+    m_int = waves_ref[...]
+    m_float = m_int.astype(jnp.float32)
     active = 2 * m_int < row_points
     parity = jnp.where((m_int & 1) == 0, 1.0, -1.0)
     factor = jnp.where(active, jnp.where(m_int == 0, 1.0, 2.0), 0.0)
@@ -100,9 +107,8 @@
     fill(lhs_sin, -factor * imag_value, -slope * real_value, -factor * imag_slope)
     scale = scales_ref[...]
 
-    @pl.loop(0, blocks)
-    def _(index):
-        at = pl.multiple_of(index * LANE, LANE)
+    for index in range(blocks):
+        at = index * LANE
         contract = (((1,), (1,)), ((), ()))
         even = lax.dot_general(lhs_cos[...], cos_tab[pl.ds(at, LANE), :], contract, preferred_element_type=jnp.float32)
         odd = lax.dot_general(lhs_sin[...], sin_tab[pl.ds(at, LANE), :], contract, preferred_element_type=jnp.float32)
@@ -138,6 +144,11 @@
             both = [real[low:low + part_rows], imag[low:low + part_rows]]
             out_ref[2 * row + term] = jnp.concatenate(both, axis=0).astype(out_ref.dtype)
 
+
+def place_values(points_ref, images, values_ref):
+    _, rows, width = images.shape
+    blocks = width // LANE
+    row_points = points_ref[0]
     flip = (
         lax.broadcasted_iota(jnp.int32, (LANE, LANE), 0) + lax.broadcasted_iota(jnp.int32, (LANE, LANE), 1) == LANE - 1
     ).astype(jnp.float32).astype(jnp.bfloat16)
@@ -159,34 +170,6 @@
     total = total + pltpu.roll(reverse(2), lax.rem(halfway - (width - 1) + NPAD, NPAD), axis=1)
     total = total + pltpu.roll(reverse(3), lax.rem(row_points - (width - 1) + NPAD, NPAD), axis=1)
     values_ref[...] = total.astype(values_ref.dtype)
-
-
-def grid_stage(four, scales, row_points, assignment):
-    _, rows, wave_count = four.shape
-    width = -(-(wave_count + 5) // LANE) * LANE
-    starts = -(-(width // LANE) // 8) * 8
-    smem, vmem = pl.BlockSpec(memory_space=pltpu.SMEM), pl.BlockSpec(memory_space=pltpu.VMEM)
-    f32, b16 = jnp.float32, jnp.bfloat16
-    return pl.pallas_call(
-        grid_kernel,
-        out_shape=(jax.ShapeDtypeStruct((4, rows, wave_count), b16), jax.ShapeDtypeStruct((rows, NPAD), b16)),
-        in_specs=[smem, vmem, vmem, vmem],
-        out_specs=(vmem, vmem),
-        scratch_shapes=[
-            pltpu.VMEM((LANE, wave_count), f32),
-            pltpu.VMEM((LANE, wave_count), f32),
-            pltpu.VMEM((starts, wave_count), f32),
-            pltpu.VMEM((starts, wave_count), f32),
-            pltpu.VMEM((width, wave_count), b16),
-            pltpu.VMEM((width, wave_count), b16),
-            pltpu.VMEM((12 * rows, wave_count), b16),
-            pltpu.VMEM((12 * rows, wave_count), b16),
-            pltpu.VMEM((4 * rows, width), b16),
-            pltpu.VMEM((4 * rows, width), b16),
-            pltpu.VMEM((4, rows, width), f32),
-        ],
-        compiler_params=pltpu.CompilerParams(vmem_limit_bytes=40 * 1024 * 1024),
-    )(row_points[None], scales, assignment[None, :], four)
 
 
 def split_column(column):
@@ -210,11 +193,15 @@
     )
 
 
-def inverse_kernel(
+def transform_kernel(
     lat_size, lev_size, pack, chunks,
-    own_ref, spec_hbm, leg_hbm, out_ref,
+    own_ref, points_ref, scales_ref, waves_ref, spec_hbm, leg_hbm, out_ref, images,
     spec, leg, lev_send, lev_recv, summed, turned, lat_send, lat_recv,
     load_sem, lev_send_sem, lev_recv_sem, lat_send_sem, lat_recv_sem,
+    four, wave_rows, base_cos, base_sin, start_cos, start_sin, cos_tab, sin_tab,
+    lhs_cos, lhs_sin, term_cos, term_sin,
+    back_send, back_recv, back_turned, grouped, all_send, all_recv,
+    back_send_sem, back_recv_sem, all_send_sem, all_recv_sem,
 ):
     lat, lev = lax.axis_index("lat"), lax.axis_index("lev")
     _, groups, columns, totals = spec.shape
@@ -239,7 +226,7 @@
         for copy in loads[chunk]:
             copy.wait()
 
-        @pl.loop(chunk * size, (chunk + 1) * size)
+        @pl.loop(chunk * size, (chunk + 1) * size, unroll=4)
         def _(group):
             tables = []
             for which in range(pack):
@@ -264,6 +251,7 @@
             )
             copy.start()
             copies.append(copy)
+    build_tables(points_ref, waves_ref, base_cos, base_sin, start_cos, start_sin, cos_tab, sin_tab)
     for chunk in range(chunks):
         for hop in range(1, lev_size):
             copies[chunk * (lev_size - 1) + hop - 1].wait_recv()
@@ -295,10 +283,19 @@
         copy.wait()
     for row in range(block):
         pieces = [lat_recv[source, row].astype(jnp.float32) for source in range(lat_size)]
-        out_ref[row] = jnp.concatenate(pieces, axis=1).astype(jnp.bfloat16)
-
-
-def direct_kernel(
+        four[row] = jnp.concatenate(pieces, axis=1).astype(jnp.bfloat16)
+    grid_rows(
+        points_ref, scales_ref, waves_ref, four, wave_rows,
+        cos_tab, sin_tab, lhs_cos, lhs_sin, term_cos, term_sin, images,
+    )
+    direct_steps(
+        lat_size, lev_size, pack, wave_rows, out_ref,
+        back_send, back_recv, back_turned, grouped, all_send, all_recv,
+        back_send_sem, back_recv_sem, all_send_sem, all_recv_sem,
+    )
+
+
+def direct_steps(
     lat_size, lev_size, pack,
     waves_ref, out_ref,
     lat_send, lat_recv, turned, grouped, lev_send, lev_recv,
@@ -312,7 +309,6 @@
         line = waves_ref[row].astype(jnp.float32)
         for peer in range(lat_size):
             lat_send[peer, row] = line[:, peer * own:(peer + 1) * own].astype(jnp.bfloat16)
-    greet(lat_size, lev_size)
     swaps = []
     for hop in range(1, lat_size):
         peer = lax.rem(lat + hop, lat_size)
@@ -340,7 +336,7 @@
     out_ref[...] = lev_recv[...]
 
 
-def tendency_kernel(own_ref, waves_ref, leg_ref, out_ref):
+def tendency_kernel(own_ref, points_ref, waves_ref, leg_ref, images, out_ref, values_ref):
     pack, size, rows, totals = leg_ref.shape
     groups = size * pl.num_programs(0)
     lev_size, _, share, lanes = waves_ref.shape
@@ -349,7 +345,11 @@
     number = lax.broadcasted_iota(jnp.int32, (1, totals), 1) + lax.axis_index("lev") * totals
     lane = lax.broadcasted_iota(jnp.int32, (1, lanes), 1) // rows
 
-    @pl.loop(0, size)
+    @pl.when(pl.program_id(0) == 0)
+    def _():
+        place_values(points_ref, images, values_ref)
+
+    @pl.loop(0, size, unroll=4)
     def _(group):
         waves = jnp.concatenate([waves_ref[peer, group] for peer in range(lev_size)], axis=0)
         spread = jnp.concatenate(
@@ -381,11 +381,18 @@
     anywhere = pl.BlockSpec(memory_space=pl.ANY)
     f32, b16 = jnp.float32, jnp.bfloat16
     dma = pltpu.SemaphoreType.DMA
-    fourier = pl.pallas_call(
-        functools.partial(inverse_kernel, lat_size, lev_size, pack, chunks),
-        out_shape=jax.ShapeDtypeStruct((block, share, wave_count), b16),
-        in_specs=[smem, anywhere, anywhere],
-        out_specs=vmem,
+    width = -(-(wave_count + 5) // LANE) * LANE
+    starts = -(-(width // LANE) // 8) * 8
+    scales = weights / points[0].astype(f32)
+    scales = jnp.repeat(scales, 4 * local_levels)[:, None]
+    gathered, images = pl.pallas_call(
+        functools.partial(transform_kernel, lat_size, lev_size, pack, chunks),
+        out_shape=(
+            jax.ShapeDtypeStruct((lev_size, groups, share, pack * rows), b16),
+            jax.ShapeDtypeStruct((4, share, width), f32),
+        ),
+        in_specs=[smem, smem, vmem, vmem, anywhere, anywhere],
+        out_specs=(vmem, vmem),
         scratch_shapes=[
             pltpu.VMEM((pack, groups, column_count, own_totals), b16),
             pltpu.VMEM((pack, groups, rows, own_totals), b16),
@@ -397,21 +404,18 @@
             pltpu.VMEM((lat_size, block, share, own_slots), b16),
             dma((chunks, 2)), dma((chunks, lev_size - 1)), dma((chunks, lev_size - 1)),
             dma((lat_size - 1,)), dma((lat_size - 1,)),
-        ],
-        compiler_params=pltpu.CompilerParams(
-            collective_id=0, has_side_effects=True, vmem_limit_bytes=40 * 1024 * 1024
-        ),
-    )(own_waves, spec_in, leg_in)
-    scales = weights / points[0].astype(jnp.float32)
-    scales = jnp.repeat(scales, 4 * local_levels)[:, None]
-    wave_rows, values = grid_stage(fourier, scales, points[0], assignment)
-    values = values.reshape(2, local_levels, 4, NPAD)
-    gathered = pl.pallas_call(
-        functools.partial(direct_kernel, lat_size, lev_size, pack),
-        out_shape=jax.ShapeDtypeStruct((lev_size, groups, share, pack * rows), b16),
-        in_specs=[vmem],
-        out_specs=vmem,
-        scratch_shapes=[
+            pltpu.VMEM((block, share, wave_count), b16),
+            pltpu.VMEM((block, share, wave_count), b16),
+            pltpu.VMEM((LANE, wave_count), f32),
+            pltpu.VMEM((LANE, wave_count), f32),
+            pltpu.VMEM((starts, wave_count), f32),
+            pltpu.VMEM((starts, wave_count), f32),
+            pltpu.VMEM((width, wave_count), b16),
+            pltpu.VMEM((width, wave_count), b16),
+            pltpu.VMEM((12 * share, wave_count), b16),
+            pltpu.VMEM((12 * share, wave_count), b16),
+            pltpu.VMEM((4 * share, width), b16),
+            pltpu.VMEM((4 * share, width), b16),
             pltpu.VMEM((lat_size, block, share, own_slots), b16),
             pltpu.VMEM((lat_size, block, share, own_slots), b16),
             pltpu.VMEM((rows, share, own_slots), f32),
@@ -421,22 +425,31 @@
             dma((lat_size - 1,)), dma((lat_size - 1,)), dma((lev_size - 1,)), dma((lev_size - 1,)),
         ],
         compiler_params=pltpu.CompilerParams(
-            collective_id=1, has_side_effects=True, vmem_limit_bytes=40 * 1024 * 1024
+            collective_id=0, has_side_effects=True, vmem_limit_bytes=60 * 1024 * 1024
         ),
-    )(wave_rows)
+    )(own_waves, points, scales, assignment[None, :], spec_in, leg_in)
     size = groups // 5
-    result = pl.pallas_call(
+    result, values = pl.pallas_call(
         tendency_kernel,
         grid=(groups // size,),
-        out_shape=jax.ShapeDtypeStruct((pack, groups, column_count, own_totals), b16),
+        out_shape=(
+            jax.ShapeDtypeStruct((pack, groups, column_count, own_totals), b16),
+            jax.ShapeDtypeStruct((share, NPAD), b16),
+        ),
         in_specs=[
+            smem,
             smem,
             pl.BlockSpec((lev_size, size, share, pack * rows), lambda step: (0, step, 0, 0)),
             pl.BlockSpec((pack, size, rows, own_totals), lambda step: (0, step, 0, 0)),
+            vmem,
         ],
-        out_specs=pl.BlockSpec((pack, size, column_count, own_totals), lambda step: (0, step, 0, 0)),
-        compiler_params=pltpu.CompilerParams(vmem_limit_bytes=40 * 1024 * 1024),
-    )(own_waves, gathered, leg_in)
+        out_specs=(
+            pl.BlockSpec((pack, size, column_count, own_totals), lambda step: (0, step, 0, 0)),
+            vmem,
+        ),
+        compiler_params=pltpu.CompilerParams(vmem_limit_bytes=60 * 1024 * 1024),
+    )(own_waves, points, gathered, leg_in, images)
+    values = values.reshape(2, local_levels, 4, NPAD)
     tendency = jnp.transpose(result.reshape(own_slots, column_count, own_totals), (0, 2, 1))
     return (tendency, values)
 

time: 76.4 us -> 59.9 us (0.78)
  the two profiles are of different devices: /device:TPU:0 before, /device:TPU:29 now
where the time goes in v3:
time: 59.9 us; the launch traced here: 59.4 us
  Pallas kernels  52.5 us (88%)
  local copies, waits for them, and re-layouts  5.02 us (8%)
  between operations  1.29 us (2%)
  other arithmetic  0.66 us (1%)
    pallas_call x1, Pallas kernels, body(): pl.pallas_call(functools.partial(transform_kernel, lat_size, lev_size, pa...  43.4 us
    pallas_call x1, Pallas kernels, body(): pl.pallas_call(tendency_kernel, grid=(groups // size,), out_shape=(jax.Sh...  9.11 us
    reshape x1, local copies, waits for them, and re-layouts, body(): values = values.reshape(2, local_levels, 4, NPAD)  1.63 us
    dynamic_slice x1, local copies, waits for them, and re-layouts, body(): lax.dynamic_slice_in_dim(assignment, lax.axis_index('lat') * own_slots, o...  1.35 us
    broadcast_in_dim x1, local copies, waits for them, and re-layouts, body(): assignment[None, :]  1.29 us

profile of v3, /device:TPU:29, one launch (start us, length us, event | category | flops | bytes accessed | tf_op | source)
XLA Modules:
  0.0 59.4 jit_solution(10028482843088072805)
XLA Ops:
  1.3 0.7 %broadcast_divide_fusion = f32[2]{0:T(128)S(1)} fusion(f32[2]{0:T(128)} %param.7, f32[]{:T(128)} %bitcast), kind=kLoop, calls=%fused_computation | loop fusion | flops 2 | bytes 20 | tf_op jit(solution)/shard_map/div | solution.py:386
  1.9 1.3 %dynamic_slice.3.own_ref = s32[160]{0:T(256)} dynamic-slice(s32[1280]{0:T(1024)} %param.9, s32[]{:T(128)S(6)} %select_n.3), dynamic_slice_sizes={160} | dynamic-slice | bytes 1284 | tf_op jit(solution)/shard_map/dynamic_slice | solution.py:377
  3.3 0.1 broadcast_in_dim.6
  3.4 1.3 %broadcast_in_dim.7.waves_ref = s32[1,1280]{1,0:T(1,128)} reshape(s32[1280]{0:T(1024)} %param.9) | data formatting | bytes 10240 | tf_op jit(solution)/shard_map/broadcast_in_dim | solution.py:430
  4.7 0.7 %broadcast_in_dim_reshape.4.scales_ref = f32[16,1]{1,0:T(8,128)} reshape(f32[2,8]{1,0:T(2,128)S(1)} %broadcast_in_dim.6) | data formatting | bytes 128 | tf_op jit(solution)/shard_map/broadcast_in_dim;reshape | solution.py:387
  5.3 43.4 %shard_map.68 = (bf16[4,40,16,128]{3,2,1,0:T(8,128)(2,1)}, f32[4,16,1408]{2,1,0:T(8,128)}) custom-call(s32[160]{0:T(256)} %dynamic_slice.3.own_ref, s32[1]{0:T(128)S(6)} %copy.8.points_ref, f32[16,1]{1,0:T(8,128)} %broadcast_in_dim_reshape.4.scales_ref, s32[1,1280]{1,0:T(1,128)} %broadcast_in_dim.7.waves_ref, bf16[4,40,64,320]{3,2,1,0:T(8,128)(2,1)} %bitcast.12, ...), custom_call_target="tpu_custom_call" | custom-call | tf_op jit(solution)/shard_map/pallas_call | solution.py:388
  48.7 9.1 %shard_map.69 = (bf16[4,40,64,320]{3,2,1,0:T(8,128)(2,1)}, bf16[16,5376]{1,0:T(8,128)(2,1)}) custom-call(s32[160]{0:T(256)} %dynamic_slice.3.own_ref, s32[1]{0:T(128)S(6)} %copy.8.points_ref, bf16[4,40,16,128]{3,2,1,0:T(8,128)(2,1)} %get-tuple-element.6.waves_ref, bf16[4,40,32,320]{3,2,1,0:T(8,128)(2,1)} %bitcast.11, f32[4,16,1408]{2,1,0:T(8,128)} %get-tuple-element.7.images), custom_call_target="tpu_custom_call" | custom-call | tf_op jit(solution)/shard_map/pallas_call | solution.py:432
  57.8 1.6 %reshape.20 = bf16[2,2,4,5376]{3,2,1,0:T(4,128)(2,1)} reshape(bf16[16,5376]{1,0:T(8,128)(2,1)} %get-tuple-element.9) | data formatting | bytes 344064 | tf_op jit(solution)/shard_map/reshape | solution.py:452

commit v4 on v3

--- a/solution.py
+++ b/solution.py
@@ -105,7 +105,8 @@
 
     fill(lhs_cos, factor * real_value, -slope * imag_value, factor * real_slope)
     fill(lhs_sin, -factor * imag_value, -slope * real_value, -factor * imag_slope)
-    scale = scales_ref[...]
+    which_row = lax.broadcasted_iota(jnp.int32, (rows, 1), 0) < part_rows
+    scale = jnp.where(which_row, scales_ref[0], scales_ref[1]) / row_points.astype(jnp.float32)
 
     for index in range(blocks):
         at = index * LANE
@@ -169,7 +170,10 @@
     total = total + pltpu.roll(straight(1), halfway, axis=1)
     total = total + pltpu.roll(reverse(2), lax.rem(halfway - (width - 1) + NPAD, NPAD), axis=1)
     total = total + pltpu.roll(reverse(3), lax.rem(row_points - (width - 1) + NPAD, NPAD), axis=1)
-    values_ref[...] = total.astype(values_ref.dtype)
+    for row in range(values_ref.shape[0]):
+        for level in range(values_ref.shape[1]):
+            low = (row * values_ref.shape[1] + level) * 4
+            values_ref[row, level] = total[low:low + 4].astype(values_ref.dtype)
 
 
 def split_column(column):
@@ -230,7 +234,7 @@
         def _(group):
             tables = []
             for which in range(pack):
-                kept = jnp.where(number >= own_ref[which * groups + group], 1.0, 0.0).astype(jnp.bfloat16)
+                kept = jnp.where(number >= own_ref[lat * pack * groups + which * groups + group], 1.0, 0.0).astype(jnp.bfloat16)
                 tables.append(leg[which, group] * kept)
             table = jnp.concatenate(tables, axis=0)
             source = jnp.concatenate([spec[which, group] for which in range(pack)], axis=0)
@@ -324,14 +328,36 @@
         flat = jnp.concatenate([line[:, which * groups:(which + 1) * groups] for which in range(pack)], axis=0)
         grouped[:, column, :] = jnp.transpose(flat)
     lev_send[...] = grouped[...].astype(jnp.bfloat16)
-    copies = []
-    for hop in range(1, lev_size):
-        peer = lax.rem(lev + hop, lev_size)
-        copy = remote(lev_send, lev_recv.at[lev], lev_send_sem.at[hop - 1], lev_recv_sem.at[hop - 1], (lat, peer))
-        copy.start()
-        copies.append(copy)
+    twin = lev + 1 - 2 * lax.rem(lev, 2)
+    far, near = [], []
+    half = groups // 2
+    for part in range(2):
+        for hop in range(1, lev_size // 2):
+            peer = lax.rem(lev + 2 * hop, lev_size)
+            index = part * (lev_size // 2) + hop
+            rows_of = pl.ds(part * half, half)
+            copy = remote(
+                lev_send.at[rows_of], lev_recv.at[lev, rows_of],
+                lev_send_sem.at[0, index], lev_recv_sem.at[0, index], (lat, peer),
+            )
+            copy.start()
+            far.append((copy, hop, index, rows_of))
+    copy = remote(lev_send, lev_recv.at[lev], lev_send_sem.at[1, 0], lev_recv_sem.at[1, 0], (lat, twin))
+    copy.start()
+    near.append(copy)
     lev_recv[lev] = lev_send[...]
-    for copy in copies:
+    for copy, hop, index, rows_of in far:
+        copy.wait_recv()
+        source = lax.rem(lev - 2 * hop + lev_size, lev_size)
+        passed = remote(
+            lev_recv.at[source, rows_of], lev_recv.at[source, rows_of],
+            lev_send_sem.at[1, index], lev_recv_sem.at[1, index], (lat, twin),
+        )
+        passed.start()
+        near.append(passed)
+    for copy, _, _, _ in far:
+        copy.wait_send()
+    for copy in near:
         copy.wait()
     out_ref[...] = lev_recv[...]
 
@@ -342,6 +368,7 @@
     lev_size, _, share, lanes = waves_ref.shape
     columns = lev_size * share
     first = pl.program_id(0) * size
+    lat = lax.axis_index("lat")
     number = lax.broadcasted_iota(jnp.int32, (1, totals), 1) + lax.axis_index("lev") * totals
     lane = lax.broadcasted_iota(jnp.int32, (1, lanes), 1) // rows
 
@@ -358,7 +385,7 @@
         table = jnp.concatenate([leg_ref[which, group] for which in range(pack)], axis=0)
         product = jnp.dot(spread, table, preferred_element_type=jnp.float32)
         for which in range(pack):
-            kept = number >= own_ref[which * groups + first + group]
+            kept = number >= own_ref[lat * pack * groups + which * groups + first + group]
             out_ref[which, group] = jnp.where(kept, product[which * columns:(which + 1) * columns], 0.0).astype(jnp.bfloat16)
 
 
@@ -374,7 +401,6 @@
     groups = own_slots // pack
     block = rows // lat_size
     chunks = 5
-    own_waves = lax.dynamic_slice_in_dim(assignment, lax.axis_index("lat") * own_slots, own_slots)
     spec_in = jnp.transpose(spectral, (0, 2, 1)).reshape(pack, groups, column_count, own_totals)
     leg_in = jnp.transpose(legendre, (0, 2, 1)).reshape(pack, groups, rows, own_totals)
     smem, vmem = pl.BlockSpec(memory_space=pltpu.SMEM), pl.BlockSpec(memory_space=pltpu.VMEM)
@@ -383,15 +409,13 @@
     dma = pltpu.SemaphoreType.DMA
     width = -(-(wave_count + 5) // LANE) * LANE
     starts = -(-(width // LANE) // 8) * 8
-    scales = weights / points[0].astype(f32)
-    scales = jnp.repeat(scales, 4 * local_levels)[:, None]
     gathered, images = pl.pallas_call(
         functools.partial(transform_kernel, lat_size, lev_size, pack, chunks),
         out_shape=(
             jax.ShapeDtypeStruct((lev_size, groups, share, pack * rows), b16),
             jax.ShapeDtypeStruct((4, share, width), f32),
         ),
-        in_specs=[smem, smem, vmem, vmem, anywhere, anywhere],
+        in_specs=[smem, smem, smem, vmem, anywhere, anywhere],
         out_specs=(vmem, vmem),
         scratch_shapes=[
             pltpu.VMEM((pack, groups, column_count, own_totals), b16),
@@ -422,19 +446,19 @@
             pltpu.VMEM((groups, share, pack * rows), f32),
             pltpu.VMEM((groups, share, pack * rows), b16),
             pltpu.VMEM((lev_size, groups, share, pack * rows), b16),
-            dma((lat_size - 1,)), dma((lat_size - 1,)), dma((lev_size - 1,)), dma((lev_size - 1,)),
+            dma((lat_size - 1,)), dma((lat_size - 1,)), dma((2, lev_size)), dma((2, lev_size)),
         ],
         compiler_params=pltpu.CompilerParams(
             collective_id=0, has_side_effects=True, vmem_limit_bytes=60 * 1024 * 1024
         ),
-    )(own_waves, points, scales, assignment[None, :], spec_in, leg_in)
+    )(assignment, points, weights, assignment[None, :], spec_in, leg_in)
     size = groups // 5
     result, values = pl.pallas_call(
         tendency_kernel,
         grid=(groups // size,),
         out_shape=(
             jax.ShapeDtypeStruct((pack, groups, column_count, own_totals), b16),
-            jax.ShapeDtypeStruct((share, NPAD), b16),
+            jax.ShapeDtypeStruct((2, local_levels, 4, NPAD), b16),
         ),
         in_specs=[
             smem,
@@ -448,8 +472,7 @@
             vmem,
         ),
         compiler_params=pltpu.CompilerParams(vmem_limit_bytes=60 * 1024 * 1024),
-    )(own_waves, points, gathered, leg_in, images)
-    values = values.reshape(2, local_levels, 4, NPAD)
+    )(assignment, points, gathered, leg_in, images)
     tendency = jnp.transpose(result.reshape(own_slots, column_count, own_totals), (0, 2, 1))
     return (tendency, values)
 

time: 59.9 us -> 53.4 us (0.89)
  the two profiles are of different devices: /device:TPU:29 before, /device:TPU:0 now
where the time goes in v4:
time: 53.4 us; the launch traced here: 52.9 us
  Pallas kernels  50.3 us (94%)
  local copies, waits for them, and re-layouts  1.3 us (2%)
  between operations  1.28 us (2%)
    pallas_call x1, Pallas kernels, body(): pl.pallas_call(functools.partial(transform_kernel, lat_size, lev_size, pa...  41.2 us
    pallas_call x1, Pallas kernels, body(): pl.pallas_call(tendency_kernel, grid=(groups // size,), out_shape=(jax.Sh...  9.15 us
    broadcast_in_dim x1, local copies, waits for them, and re-layouts, body(): assignment[None, :]  1.3 us

profile of v4, /device:TPU:0, one launch (start us, length us, event | category | flops | bytes accessed | tf_op | source)
XLA Modules:
  0.0 52.9 jit_solution(17973113724156783960)
XLA Ops:
  1.3 1.3 %broadcast_in_dim.3.waves_ref = s32[1,1280]{1,0:T(1,128)} reshape(s32[1280]{0:T(1024)} %own_ref.3) | data formatting | bytes 10240 | tf_op jit(solution)/shard_map/broadcast_in_dim | solution.py:454
  2.6 41.2 %shard_map.68 = (bf16[4,40,16,128]{3,2,1,0:T(8,128)(2,1)}, f32[4,16,1408]{2,1,0:T(8,128)}) custom-call(s32[1280]{0:T(1024)} %own_ref.3, s32[1]{0:T(128)S(6)} %copy.7.points_ref, f32[2]{0:T(128)} %scales_ref.1, s32[1,1280]{1,0:T(1,128)} %broadcast_in_dim.3.waves_ref, bf16[4,40,64,320]{3,2,1,0:T(8,128)(2,1)} %bitcast.11, bf16[4,40,32,320]{3,2,1,0:T(8,128)(2,1)} %bitcast.9), custom_call_target="tpu_custom_call" | custom-call | tf_op jit(solution)/shard_map/pallas_call | solution.py:412
  43.8 9.2 %shard_map.69 = (bf16[4,40,64,320]{3,2,1,0:T(8,128)(2,1)}, bf16[2,2,4,5376]{3,2,1,0:T(4,128)(2,1)}) custom-call(s32[1280]{0:T(1024)} %own_ref.3, s32[1]{0:T(128)S(6)} %copy.7.points_ref, bf16[4,40,16,128]{3,2,1,0:T(8,128)(2,1)} %get-tuple-element.6.waves_ref, bf16[4,40,32,320]{3,2,1,0:T(8,128)(2,1)} %bitcast.10, f32[4,16,1408]{2,1,0:T(8,128)} %get-tuple-element.7.images), custom_call_target="tpu_custom_call" | custom-call | tf_op jit(solution)/shard_map/pallas_call | solution.py:456
